TPU v7x, 256 devices: a whole 4x4x8 slice. The times are simulated.
256 devices in a mesh: ctx: 16 (over y_hi, z), tp: 8 (over x, core), grp: 2 (over y_lo).
Axes of the slice: x: 4, y: 4 (y_hi: 2, y_lo: 2; y = y_hi * 2 + y_lo), z: 8, core: 2. Of those that a mesh axis runs over, the one named last changes fastest.
Arguments:
- span_queries: bfloat16 [2, 1024, 8192], P('grp', 'ctx', 'tp'), may hold values from -100 to 100
- span_keys: bfloat16 [2, 1024, 1024], P('grp', 'ctx', 'tp'), may hold values from -7 to 7
- span_values: bfloat16 [2, 1024, 1024], P('grp', 'ctx', 'tp'), may hold values from -6 to 6
- prompt_keys: bfloat16 [2, 32768, 1024], P('grp', 'ctx', 'tp'), may hold values from -7 to 7
- prompt_values: bfloat16 [2, 32768, 1024], P('grp', 'ctx', 'tp'), may hold values from -6 to 6
- block_owner: int32 [2, 64], replicated, may hold values from 0 to 15, as said below
- block_slot: int32 [2, 64], replicated, may hold values from 0 to 7, as said below
- decode_queries: bfloat16 [2, 256, 4, 8192], P('grp', 'ctx', None, 'tp'), may hold values from -100 to 100
- decode_new_keys: bfloat16 [2, 256, 4, 1024], P('grp', 'ctx', None, 'tp'), may hold values from -8 to 8
- decode_new_values: bfloat16 [2, 256, 4, 1024], P('grp', 'ctx', None, 'tp'), may hold values from -6 to 6
- cache_keys: bfloat16 [2, 256, 256, 1024], P('grp', 'ctx', None, 'tp'), may hold values from -7 to 7
- cache_values: bfloat16 [2, 256, 256, 1024], P('grp', 'ctx', None, 'tp'), may hold values from -6 to 6
- cache_len: int32 [2, 256], P('grp', 'ctx'), may hold values from 64 to 256, as said below
- out_weight: bfloat16 [8192, 4096], P('tp'), may hold values from -0.0625 to 0.0625
Outputs:
- prefill_out: bfloat16 [2, 1024, 4096], P('grp', ('ctx', 'tp'))
- decode_out: bfloat16 [2, 256, 4, 4096], P('grp', ('ctx', 'tp'))
Inputs may be any that keep to these rules, and one draw needn't show every extreme that they name: `block_owner`: in each pool at most 8 blocks name one replica, and exactly 8 blocks name some replica. `block_slot`: blocks of one pool that name the same replica have different slots. `cache_len`: some row of each pool has 256 live slots.
All inputs are finite; a program needn't handle non-finite values.
Results may differ from a plain program's by a relative error of at most 0.02.
Values may be sent and summed in bfloat16 or wider, within the bound.
A program may use at most 128 MiB of HBM per device.

v0:
```python
import math

import jax
import jax.numpy as jnp
from jax import lax
from jax.sharding import PartitionSpec as P

HD = 128
BLOCK = 16
SLOTS = 8


def from_behind(block, axis, distance):
    devices = range(lax.axis_size(axis))
    route = [((i - distance) % len(devices), i) for i in devices]
    return lax.ppermute(block, axis, route)


def attend_block(softmax_state, queries, key_rows, value_rows, key_start, query_pos, score_scale):
    key_count = key_rows.shape[0]
    kvh_dev = queries.shape[1]
    head_size = queries.shape[3]
    block_width = math.gcd(key_count, 2048)
    block_count = key_count // block_width
    key_blocks = key_rows.reshape(block_count, block_width, kvh_dev, head_size)
    value_blocks = value_rows.reshape(block_count, block_width, kvh_dev, head_size)

    def advance(running_state, inputs):
        running, weight_sum, accum = running_state
        block_keys, block_values, block_index = inputs
        scores = (
            jnp.einsum("tkgd,skd->tkgs", queries, block_keys, preferred_element_type=jnp.float32)
            * score_scale
        )
        key_pos = key_start + block_index * block_width + jnp.arange(block_width, dtype=jnp.int32)
        visible = (key_pos[None, :] <= query_pos[:, None])[:, None, None, :]
        scores = jnp.where(visible, scores, -1e30)
        highest = jnp.maximum(running, jnp.max(scores, axis=-1))
        weights = jnp.where(visible, jnp.exp(scores - highest[..., None]), 0.0)
        rescale = jnp.exp(running - highest)
        weight_sum = weight_sum * rescale + jnp.sum(weights, axis=-1)
        accum = accum * rescale[..., None] + jnp.einsum(
            "tkgs,skd->tkgd",
            weights.astype(jnp.bfloat16),
            block_values,
            preferred_element_type=jnp.float32,
        )
        return ((highest, weight_sum, accum), None)

    final_state, ignored = lax.scan(
        advance, softmax_state, (key_blocks, value_blocks, jnp.arange(block_count, dtype=jnp.int32))
    )
    return final_state


def decode_attend(
    queries, cache_k, cache_v, lengths, slot_k, slot_v, occupied, new_k, new_v, score_scale
):
    cache_size = cache_k.shape[1]
    step_count = queries.shape[1]
    score_cache = (
        jnp.einsum("rtkgd,rckd->rtkgc", queries, cache_k, preferred_element_type=jnp.float32)
        * score_scale
    )
    score_slot = (
        jnp.einsum("rtkgd,skd->rtkgs", queries, slot_k, preferred_element_type=jnp.float32)
        * score_scale
    )
    score_new = (
        jnp.einsum("rtkgd,rukd->rtkgu", queries, new_k, preferred_element_type=jnp.float32)
        * score_scale
    )
    see_cache = (jnp.arange(cache_size, dtype=jnp.int32)[None, :] < lengths[:, None])[
        :, None, None, None, :
    ]
    see_slot = occupied[None, None, None, None, :]
    step_ids = jnp.arange(step_count, dtype=jnp.int32)
    see_new = (step_ids[None, :] <= step_ids[:, None])[None, :, None, None, :]
    score_cache = jnp.where(see_cache, score_cache, -1e30)
    score_slot = jnp.where(see_slot, score_slot, -1e30)
    score_new = jnp.where(see_new, score_new, -1e30)
    highest = jnp.maximum(
        jnp.maximum(jnp.max(score_cache, axis=-1), jnp.max(score_slot, axis=-1)),
        jnp.max(score_new, axis=-1),
    )
    weight_cache = jnp.where(see_cache, jnp.exp(score_cache - highest[..., None]), 0.0)
    weight_slot = jnp.where(see_slot, jnp.exp(score_slot - highest[..., None]), 0.0)
    weight_new = jnp.where(see_new, jnp.exp(score_new - highest[..., None]), 0.0)
    weight_sum = (
        jnp.sum(weight_cache, axis=-1)
        + jnp.sum(weight_slot, axis=-1)
        + jnp.sum(weight_new, axis=-1)
    )
    blended = jnp.einsum(
        "rtkgc,rckd->rtkgd",
        weight_cache.astype(jnp.bfloat16),
        cache_v,
        preferred_element_type=jnp.float32,
    )
    blended = blended + jnp.einsum(
        "rtkgs,skd->rtkgd",
        weight_slot.astype(jnp.bfloat16),
        slot_v,
        preferred_element_type=jnp.float32,
    )
    blended = blended + jnp.einsum(
        "rtkgu,rukd->rtkgd",
        weight_new.astype(jnp.bfloat16),
        new_v,
        preferred_element_type=jnp.float32,
    )
    return (blended / weight_sum[..., None]).astype(jnp.bfloat16)


def on_device(
    span_queries,
    span_keys,
    span_values,
    prompt_keys,
    prompt_values,
    block_owner,
    block_slot,
    decode_queries,
    decode_new_keys,
    decode_new_values,
    cache_keys,
    cache_values,
    cache_len,
    out_weight,
):
    ctx_count = lax.axis_size("ctx")
    tp_count = lax.axis_size("tp")
    replica = lax.axis_index("ctx")
    pool_index = lax.axis_index("grp")
    kvh_dev = span_keys.shape[-1] // HD
    heads_dev = span_queries.shape[-1] // HD
    group_size = heads_dev // kvh_dev
    score_scale = HD ** (-0.5)
    token_count = span_queries.shape[1]
    prompt_dev = prompt_keys.shape[1]
    prompt_total = prompt_dev * ctx_count
    queries = span_queries[0].reshape(token_count, kvh_dev, group_size, HD)
    span_k = span_keys[0]
    span_v = span_values[0]
    prompt_k = prompt_keys[0]
    prompt_v = prompt_values[0]
    start_state = (
        jnp.full((token_count, kvh_dev, group_size), -1e30, jnp.float32),
        jnp.zeros((token_count, kvh_dev, group_size), jnp.float32),
        jnp.zeros((token_count, kvh_dev, group_size, HD), jnp.float32),
    )
    own_pos = prompt_total + replica * token_count + jnp.arange(token_count, dtype=jnp.int32)
    shard_piece = (
        lax.all_gather(prompt_k, "ctx", axis=0, tiled=True),
        lax.all_gather(prompt_v, "ctx", axis=0, tiled=True),
    )
    softmax_state = attend_block(
        start_state, queries, shard_piece[0], shard_piece[1], jnp.int32(0), own_pos, score_scale
    )
    shard_piece = (
        lax.all_gather(span_k, "ctx", axis=0, tiled=True),
        lax.all_gather(span_v, "ctx", axis=0, tiled=True),
    )
    running, weight_sum, accum = attend_block(
        softmax_state,
        queries,
        shard_piece[0],
        shard_piece[1],
        prompt_total + jnp.int32(0),
        own_pos,
        score_scale,
    )
    attention = (
        (accum / weight_sum[..., None]).astype(jnp.bfloat16).reshape(token_count, heads_dev * HD)
    )
    row_block = attention
    prefill_part = lax.psum_scatter(
        jnp.dot(row_block, out_weight, preferred_element_type=jnp.float32).astype(jnp.bfloat16),
        "tp",
        scatter_dimension=0,
        tiled=True,
    ).astype(jnp.float32)
    prefill_out = prefill_part.astype(jnp.bfloat16).reshape(
        1, token_count // tp_count, prefill_part.shape[-1]
    )
    source_pool = 1 - pool_index
    slot_range = jnp.arange(SLOTS, dtype=jnp.int32)
    owner_ids = lax.dynamic_index_in_dim(block_owner, source_pool, 0, keepdims=False)
    slot_ids = lax.dynamic_index_in_dim(block_slot, source_pool, 0, keepdims=False)
    incoming = (owner_ids[None, :] == replica) & (slot_ids[None, :] == slot_range[:, None])
    occupied = jnp.repeat(jnp.any(incoming, axis=1), BLOCK)
    flat_width = BLOCK * kvh_dev * HD
    arrived_k, arrived_v = from_behind((span_k, span_v), "grp", 1)
    shard_piece = (
        lax.all_gather(arrived_k, "ctx", axis=0, tiled=True),
        lax.all_gather(arrived_v, "ctx", axis=0, tiled=True),
    )
    block_amount = shard_piece[0].shape[0] // BLOCK
    picked = incoming.astype(jnp.bfloat16)
    key_sum = jnp.dot(
        picked, shard_piece[0].reshape(block_amount, flat_width), preferred_element_type=jnp.float32
    )
    value_sum = jnp.dot(
        picked, shard_piece[1].reshape(block_amount, flat_width), preferred_element_type=jnp.float32
    )
    slot_k = key_sum.astype(jnp.bfloat16)
    slot_v = value_sum.astype(jnp.bfloat16)
    row_count = decode_queries.shape[1]
    step_count = decode_queries.shape[2]
    dec_queries = decode_queries[0].reshape(row_count, step_count, kvh_dev, group_size, HD)
    dec_cache_k = cache_keys[0].reshape(row_count, cache_keys.shape[2], kvh_dev, HD)
    dec_cache_v = cache_values[0].reshape(row_count, cache_values.shape[2], kvh_dev, HD)
    dec_new_k = decode_new_keys[0].reshape(row_count, step_count, kvh_dev, HD)
    dec_new_v = decode_new_values[0].reshape(row_count, step_count, kvh_dev, HD)
    slot_keys = slot_k.reshape(SLOTS * BLOCK, kvh_dev, HD)
    slot_values = slot_v.reshape(SLOTS * BLOCK, kvh_dev, HD)
    decoded = decode_attend(
        dec_queries,
        dec_cache_k,
        dec_cache_v,
        cache_len[0],
        slot_keys,
        slot_values,
        occupied,
        dec_new_k,
        dec_new_v,
        score_scale,
    )
    decoded = decoded.reshape(row_count * step_count, heads_dev * HD)
    row_block = decoded
    decode_part = lax.psum_scatter(
        jnp.dot(row_block, out_weight, preferred_element_type=jnp.float32).astype(jnp.bfloat16),
        "tp",
        scatter_dimension=0,
        tiled=True,
    ).astype(jnp.float32)
    decode_out = decode_part.astype(jnp.bfloat16).reshape(
        1, row_count // tp_count, step_count, decode_part.shape[-1]
    )
    return (prefill_out, decode_out)


def solution(mesh):
    in_specs = (
        P("grp", "ctx", "tp"),
        P("grp", "ctx", "tp"),
        P("grp", "ctx", "tp"),
        P("grp", "ctx", "tp"),
        P("grp", "ctx", "tp"),
        P(),
        P(),
        P("grp", "ctx", None, "tp"),
        P("grp", "ctx", None, "tp"),
        P("grp", "ctx", None, "tp"),
        P("grp", "ctx", None, "tp"),
        P("grp", "ctx", None, "tp"),
        P("grp", "ctx"),
        P("tp", None),
    )
    out_specs = (P("grp", ("ctx", "tp"), None), P("grp", ("ctx", "tp"), None, None))
    return jax.shard_map(
        on_device, mesh=mesh, in_specs=in_specs, out_specs=out_specs, check_vma=False
    )
```

profile of v0, /device:TPU:1, one launch (start us, length us, event | category | flops | bytes accessed | tf_op | source)
XLA Modules:
  0.0 455.7 jit_solution(7544124545642590508)
XLA Ops:
  9.5 2.2 collective-permute-start.1
  15.2 38.8 %all-gather.2 = bf16[1,1024,128]{2,1,0:T(8,128)(2,1)S(1)} all-gather(bf16[1,64,128]{2,1,0:T(8,128)(2,1)} %param.17), channel_id=4, replica_groups=mesh['ctx'=16,'tp'=8,'grp'=2] {'ctx'}, dimensions={1}, use_global_device_ids=true | all-gather | bytes 278528 | tf_op jit(solution)/shard_map/all_gather | solution.py:161
  54.0 33.8 %all-gather.3 = bf16[1,1024,128]{2,1,0:T(8,128)(2,1)} all-gather(bf16[1,64,128]{2,1,0:T(8,128)(2,1)} %param.18), channel_id=5, replica_groups=mesh['ctx'=16,'tp'=8,'grp'=2] {'ctx'}, dimensions={1}, use_global_device_ids=true | all-gather | bytes 278528 | tf_op jit(solution)/shard_map/all_gather | solution.py:162
  88.6 2.7 fusion.101
  94.7 34.7 %all_gather.22 = bf16[1024,128]{1,0:T(8,128)(2,1)} all-gather(bf16[64,128]{1,0:T(8,128)(2,1)} %collective-permute-done), channel_id=1, replica_groups=mesh['ctx'=16,'tp'=8,'grp'=2] {'ctx'}, dimensions={0}, use_global_device_ids=true | all-gather | bytes 278528 | tf_op jit(solution)/shard_map/all_gather | solution.py:195
  132.3 35.2 %all_gather.23 = bf16[1024,128]{1,0:T(8,128)(2,1)} all-gather(bf16[64,128]{1,0:T(8,128)(2,1)} %collective-permute-done.1), channel_id=1, replica_groups=mesh['ctx'=16,'tp'=8,'grp'=2] {'ctx'}, dimensions={0}, use_global_device_ids=true | all-gather | bytes 278528 | tf_op jit(solution)/shard_map/all_gather | solution.py:196
  181.1 5.8 %convolution_convert_fusion = bf16[64,4096]{1,0:T(8,128)(2,1)} fusion(bf16[1024,4096]{1,0:T(8,128)(2,1)} %param.29, bf16[8,8,8,128]{3,2,1,0:T(8,128)(2,1)S(1)} %bitcast.287), kind=kOutput, calls=%fused_computation.31 | convolution fusion | flops 537133056 | bytes 9043968 | tf_op jit(solution)/shard_map/dot_general | solution.py:232
  187.2 102.6 %all-gather.9.cloned.1.call-done = bf16[1,32768,128]{2,1,0:T(8,128)(2,1)} async-done(((bf16[1,2048,128]{2,1,0:T(8,128)(2,1)}), bf16[1,32768,128]{2,1,0:T(8,128)(2,1)}) %all-gather.9.cloned.1.call-update) | async-done | bytes 8388624 | tf_op jit(solution)/shard_map/all_gather | solution.py:155
  289.8 121.9 %while.3 = (s32[]{:T(128)}, f32[64,1,8]{0,2,1:T(8,128)S(1)}, f32[64,1,8]{0,2,1:T(8,128)S(1)}, f32[64,1,8,128]{3,0,2,1:T(8,128)}, s32[16]{0:T(128)S(1)}, /*index=...) while((s32[]{:T(128)}, f32[64,1,8]{0,2,1:T(8,128)S(1)}, ...), condition=%wide.region_3.4_spmd.clone, body=%wide.region_0.3_spmd.clone.sunk | while | flops 550835264 | bytes 16958184 | solution.py:50
  302.1 2.2 fusion.121
  309.7 2.2 fusion.121
  324.9 2.2 fusion.121
  332.5 2.2 fusion.121
  340.2 2.2 fusion.121
  347.8 2.2 fusion.121
  355.4 2.2 fusion.121
  363.0 2.2 fusion.121
  370.6 2.2 fusion.121
  385.9 2.2 fusion.121
  393.5 2.2 fusion.121
  401.1 2.2 fusion.121
  408.7 2.2 fusion.121
  414.1 5.7 %convolution_convert_fusion.1 = bf16[64,4096]{1,0:T(8,128)(2,1)} fusion(bf16[1024,4096]{1,0:T(8,128)(2,1)} %param.29, bf16[8,8,8,128]{3,2,1,0:T(8,128)(2,1)S(1)} %bitcast.285), kind=kOutput, calls=%fused_computation.32 | convolution fusion | flops 537133056 | bytes 9043968 | tf_op jit(solution)/shard_map/dot_general | solution.py:178
  421.4 26.9 %reduce-scatter.3.cloned.1.call-done = bf16[8,4096]{1,0:T(8,128)(2,1)} async-done(((bf16[64,4096]{1,0:T(8,128)(2,1)}), bf16[8,4096]{1,0:T(8,128)(2,1)}) %reduce-scatter.3.cloned.1.call-update) | async-done | bytes 65552 | tf_op jit(solution)/shard_map/reduce_scatter | solution.py:177
  (279 shorter events, 111.7 us)
Async XLA Ops:
  8.0 83.3 %copy-start = (bf16[1,16,256,128]{3,2,1,0:T(8,128)(2,1)S(1)}, bf16[1,16,256,128]{3,2,1,0:T(8,128)(2,1)}, u32[]{:S(2)}) copy-start(bf16[1,16,256,128]{3,2,1,0:T(8,128)(2,1)} %param.26) | copy-start | bytes 3145732
  8.0 179.2 %all-gather.7.cloned.1.call-start = ((), (), s32[]{:S(2)}) async-start(), calls=%async_computation.4 | async-start | bytes 8912896 | tf_op jit(solution)/shard_map/all_gather | solution.py:154
  8.7 281.0 %all-gather.9.cloned.1.call-start = ((), (), s32[]{:S(2)}) async-start(), calls=%async_computation.5 | async-start | bytes 8912896 | tf_op jit(solution)/shard_map/all_gather | solution.py:155
  9.5 410.4 %reduce-scatter.5.cloned.1.call-start = ((), (), s32[]{:S(2)}) async-start(), calls=%async_computation.3 | async-start | bytes 589824 | tf_op jit(solution)/shard_map/reduce_scatter | solution.py:231
  9.5 122.7 %collective-permute-start.1 = (bf16[64,128]{1,0:T(8,128)(2,1)}, bf16[64,128]{1,0:T(8,128)(2,1)}, u32[]{:S(2)}, u32[]{:S(2)}) collective-permute-start(bf16[64,128]{1,0:T(8,128)(2,1)} %bitcast.297), channel_id=1, source_target_pairs={{1,0},{0,1},{3,2},{2,3},{5,4},{4,5},{7,6},{6,7},{9,8},{8,9},{11,10... | collective-permute-start | bytes 49160 | tf_op jit(solution)/shard_map/ppermute | solution.py:16
  11.8 82.9 %collective-permute-start = (bf16[64,128]{1,0:T(8,128)(2,1)}, bf16[64,128]{1,0:T(8,128)(2,1)}, u32[]{:S(2)}, u32[]{:S(2)}) collective-permute-start(bf16[64,128]{1,0:T(8,128)(2,1)} %bitcast.296), channel_id=1, source_target_pairs={{1,0},{0,1},{3,2},{2,3},{5,4},{4,5},{7,6},{6,7},{9,8},{8,9},{11,10... | collective-permute-start | bytes 49160 | tf_op jit(solution)/shard_map/ppermute | solution.py:16
  13.8 80.9 %copy-start.5 = (pred[4,4]{1,0:T(4,128)(4,1)}, pred[4,4]{1,0:T(4,128)(4,1)S(1)}, u32[]{:S(2)}) copy-start(pred[4,4]{1,0:T(4,128)(4,1)S(1)} %iota_compare_fusion.2) | copy-start | bytes 52
  14.5 79.4 %copy-start.3 = (pred[64]{0:T(512)(128)(4,1)}, pred[64]{0:T(512)(128)(4,1)S(1)}, u32[]{:S(2)}) copy-start(pred[64]{0:T(512)(128)(4,1)S(1)} %compare_bitcast_fusion) | copy-start | bytes 196
  15.2 79.5 %copy-start.4 = (s32[64]{0:T(128)}, s32[64]{0:T(128)S(1)}, u32[]{:S(2)}) copy-start(s32[64]{0:T(128)S(1)} %dynamic-slice_bitcast_fusion) | copy-start | bytes 772
  88.6 6.0 %copy-start.1 = (pred[64,1024]{1,0:T(8,128)(4,1)}, pred[64,1024]{1,0:T(8,128)(4,1)S(1)}, u32[]{:S(2)}) copy-start(pred[64,1024]{1,0:T(8,128)(4,1)S(1)} %broadcast_compare_fusion.1) | copy-start | bytes 196612
  186.9 261.4 %reduce-scatter.3.cloned.1.call-start = ((), (), s32[]{:S(2)}) async-start(), calls=%async_computation.2 | async-start | bytes 589824 | tf_op jit(solution)/shard_map/reduce_scatter | solution.py:177
  289.7 121.9 %copy-start.2 = (pred[64,1024]{1,0:T(8,128)(4,1)S(1)}, pred[64,1024]{1,0:T(8,128)(4,1)}, u32[]{:S(2)}) copy-start(pred[64,1024]{1,0:T(8,128)(4,1)} %copy-done.1) | copy-start | bytes 196612
  291.2 3.3 copy-start.6
  298.8 3.3 copy-start.6
  314.0 3.3 copy-start.6
  321.6 3.3 copy-start.6
  329.2 3.3 copy-start.6
  336.9 3.3 copy-start.6
  352.1 3.3 copy-start.6
  367.3 3.3 copy-start.6
  374.9 3.3 copy-start.6
  382.6 3.3 copy-start.6
  390.2 3.3 copy-start.6
  397.8 3.3 copy-start.6
  (20 other events, 24.5 us)
Sparse Core Ops, SparseCore 0:
  11.8 144.9 all-gather.6
  159.7 129.9 all-gather.8
Sparse Core Ops, SparseCore 1:
  187.0 56.1 reduce-scatter.4
  420.0 28.3 reduce-scatter.2
where the time goes:
time: 459 us; the launch traced here: 456 us
  blocking collectives  142 us (31%)
  waiting for transfers between devices  131 us (29%)
  matrix products  92.9 us (20%)
  other arithmetic  30 us (7%)
  local copies, waits for them, and re-layouts  29.6 us (6%)
  between operations  15.7 us (3%)
  loops' own time  11.5 us (3%)
    all_gather x1, waiting for transfers between devices, on_device(): lax.all_gather(prompt_v, 'ctx', axis=0, tiled=True)  103 us
    all_gather x1, blocking collectives, on_device(): lax.all_gather(span_k, 'ctx', axis=0, tiled=True)  38.8 us
    dot_general x17, matrix products, advance(): jnp.einsum('tkgs,skd->tkgd', weights.astype(jnp.bfloat16), block_values,...  36.9 us
    all_gather x1, blocking collectives, on_device(): lax.all_gather(arrived_v, 'ctx', axis=0, tiled=True)  35.2 us
    all_gather x1, blocking collectives, on_device(): lax.all_gather(arrived_k, 'ctx', axis=0, tiled=True)  34.7 us
    all_gather x1, blocking collectives, on_device(): lax.all_gather(span_v, 'ctx', axis=0, tiled=True)  33.8 us
    dot_general x17, matrix products, advance(): jnp.einsum('tkgd,skd->tkgs', queries, block_keys, preferred_element_type=...  32.3 us
    reduce_scatter x2, waiting for transfers between devices, on_device(): lax.psum_scatter(jnp.dot(row_block, out_weight, preferred_element_type=jn...  26.9 us
  transfers between devices with their start and end apart: 6, of which 2 were waited for; matrix products, arithmetic and copies ran while one was open for 31% of the time, Pallas kernels for 0%

commit v1 on v0

v1 whole, which is shorter than its diff:
```python
import math

import jax
import jax.numpy as jnp
from jax import lax
from jax.experimental import pallas as pl
from jax.experimental.pallas import tpu as pltpu
from jax.sharding import PartitionSpec as P

HD = 128
BLOCK = 16
SLOTS = 8
HEADS_DEV = 8
PIECES = 8
NEG = -1e30
SCALE2 = HD**-0.5 * math.log2(math.e)
MESH = pl.DeviceIdType.MESH
BF = jnp.bfloat16
F32 = jnp.float32


def dot_nt(a, b):
    return lax.dot_general(a, b, (((1,), (1,)), ((), ())), preferred_element_type=F32)


def dot_nn(a, b):
    return jnp.dot(a, b, preferred_element_type=F32)


def split_query(q):
    scaled = q.astype(F32) * SCALE2
    high = scaled.astype(BF)
    low = (scaled - high.astype(F32)).astype(BF)
    return jnp.concatenate([high, low], axis=1)


def kernel(
    ring, tp_count,
    q_ref, sk_ref, sv_ref, pk_ref, pv_ref, owner_ref, slot_ref, dq_ref, dk_ref, dv_ref, ck_hbm, cv_hbm, len_ref, w_hbm,
    pout_ref, dout_ref,
    qall, skv, skv_par, gath, rel, par, k_own, v_own, k_par, v_par,
    acc, mx, sm, in_m, in_l, obuf, sbuf, oin, sin,
    w, ck, cv, att, part, got,
    q_send, q_recv, s_send, s_recv, sp_send, sp_recv, g_send, g_recv, r_send, r_recv, f_send, f_recv,
    o_send, o_recv, st_send, st_recv, p_send, p_recv, load,
):
    me = lax.axis_index("ctx")
    pool = lax.axis_index("grp")
    tp = lax.axis_index("tp")
    y_hi = me // ring
    z = me % ring
    y = y_hi * 2 + pool
    tokens = q_ref.shape[0]
    rows = tokens * HEADS_DEV
    prompt = pk_ref.shape[0]
    chunk = prompt // 4

    def along_z(step):
        return {"ctx": y_hi * ring + (z + step + ring) % ring}

    def along_y(step):
        there = (y + step + 4) % 4
        return {"ctx": (there // 2) * ring + z, "grp": there % 2}

    def remote(src, dst, send, recv, device):
        return pltpu.make_async_remote_copy(
            src_ref=src, dst_ref=dst, send_sem=send, recv_sem=recv, device_id=device, device_id_type=MESH
        )

    barrier = pltpu.get_barrier_semaphore()
    for device in (along_z(1), along_z(-1), along_y(1), along_y(-1)):
        pl.semaphore_signal(barrier, inc=1, device_id=device, device_id_type=MESH)
    for k in range(1, tp_count):
        pl.semaphore_signal(barrier, inc=1, device_id={"tp": (tp + k) % tp_count}, device_id_type=MESH)
    pl.semaphore_wait(barrier, 4 + tp_count - 1)

    def way(i):
        return 2 * (i % 2) - 1

    def source_z(i):
        return (z - way(i) * ((i + 1) // 2) + ring) % ring

    def query_copy(i, src):
        return remote(src, qall.at[i], q_send.at[i], q_recv.at[i], along_z(way(i)))

    def span_copy(k):
        return remote(skv, gath.at[z, y_hi], s_send.at[k], s_recv.at[k], along_y(1 - 2 * k))

    def span_relay():
        return remote(gath.at[z, ((y + 3) % 4) // 2], skv_par, sp_send.at[0], sp_recv.at[0], along_y(1))

    def gather_copy(i, at):
        return remote(gath.at[at], gath.at[at], g_send.at[i], g_recv.at[i], along_z(way(i)))

    def piece_rows(p):
        return (p % 2) * 2 * chunk + (p // 4) * chunk

    def piece_copy(p):
        src = (pk_ref if (p // 2) % 2 == 0 else pv_ref).at[pl.ds(piece_rows(p), chunk)]
        return remote(src, rel.at[p], r_send.at[p], r_recv.at[p], along_y(1 - 2 * (p % 2)))

    def piece_relay(p):
        return remote(rel.at[p], par.at[p], f_send.at[p], f_recv.at[p], along_y(1 - 2 * (p % 2)))

    def forward_piece(p):
        remote(rel.at[p], rel.at[p], r_send.at[p], r_recv.at[p], along_y(1)).wait_recv()
        piece_relay(p).start()

    query_copy(1, q_ref).start()
    query_copy(2, q_ref).start()
    skv[0:tokens, :] = sk_ref[...]
    skv[tokens : 2 * tokens, :] = sv_ref[...]
    span_copy(0).start()
    span_copy(1).start()
    for p in range(PIECES):
        piece_copy(p).start()
    loads = [
        pltpu.make_async_copy(ck_hbm, ck, load.at[0]),
        pltpu.make_async_copy(cv_hbm, cv, load.at[1]),
        pltpu.make_async_copy(w_hbm, w, load.at[2]),
    ]
    for item in loads:
        item.start()

    qall[0] = q_ref[...]
    k_own[:, 0:HD] = pk_ref[...]
    k_own[:, HD : 2 * HD] = pk_ref[...]
    v_own[:, 0:HD] = pv_ref[...]
    v_own[:, HD : 2 * HD] = jnp.ones((prompt, HD), BF)
    v_par[:, HD : 2 * HD] = jnp.ones((v_par.shape[0], HD), BF)

    half_heads = HEADS_DEV // 2
    half = tokens * half_heads

    def unit_queries(i, b):
        parts = [qall[i, :, (b * half_heads + h) * HD : (b * half_heads + h + 1) * HD] for h in range(half_heads)]
        return split_query(jnp.concatenate(parts, axis=0))

    def attend_own(i):
        for b in range(2):
            at = pl.ds(b * half, half)
            scores = dot_nt(unit_queries(i, b), k_own[...])
            top = jnp.max(scores, axis=1, keepdims=True)
            out = dot_nn(jnp.exp2(scores - top).astype(BF), v_own[...])
            mx[i, at, :] = jnp.broadcast_to(top, (half, HD))
            acc[i, at, :] = out[:, 0:HD]
            sm[i, at, :] = out[:, HD : 2 * HD]

    def attend_partner(i):
        query_ctx = y_hi * ring + source_z(i)
        partner = (1 - y_hi) * ring + z
        for b in range(2):
            at = pl.ds(b * half, half)
            scores = dot_nt(unit_queries(i, b), k_par[...])
            token = lax.broadcasted_iota(jnp.int32, (half, 2 * tokens), 0) % tokens
            key = lax.broadcasted_iota(jnp.int32, (half, 2 * tokens), 1)
            key_pos = jnp.where(key < tokens, me * tokens + key, partner * tokens + key - tokens)
            span = jnp.where(key_pos <= query_ctx * tokens + token, scores[:, prompt:], NEG)
            before = mx[i, at, 0:1]
            top = jnp.maximum(
                jnp.max(scores[:, 0:prompt], axis=1, keepdims=True), jnp.max(span, axis=1, keepdims=True)
            )
            top = jnp.maximum(top, before)
            weights = jnp.concatenate(
                [jnp.exp2(scores[:, 0:prompt] - top).astype(BF), jnp.exp2(span - top).astype(BF)], axis=1
            )
            out = dot_nn(weights, v_par[...])
            keep = jnp.exp2(before - top)
            mx[i, at, :] = jnp.broadcast_to(top, (half, HD))
            acc[i, at, :] = acc[i, at, :] * keep + out[:, 0:HD]
            sm[i, at, :] = sm[i, at, :] * keep + out[:, HD : 2 * HD]

    attend_own(0)

    for k in range(2):
        span_copy(k).wait_recv()
    span_relay().start()
    gather_copy(1, z).start()
    gather_copy(2, z).start()

    def own_step(i, carry):
        query_copy(i, qall.at[i]).wait_recv()

        @pl.when(i + 2 < ring)
        def _():
            query_copy(i + 2, qall.at[i]).start()

        attend_own(i)
        forward_piece(i - 1)
        at = source_z(i)
        gather_copy(i, at).wait_recv()

        @pl.when(i + 2 < ring)
        def _():
            gather_copy(i + 2, at).start()

        return carry

    lax.fori_loop(1, ring, own_step, 0)
    for p in range(ring - 1, PIECES):
        forward_piece(p)

    def project(which):
        width = part.shape[3]
        each = tokens // tp_count
        step = min(512, width)

        def columns(j, carry):
            at = pl.multiple_of(j * step, step)
            first = dot_nn(att[...], w[:, pl.ds(at, step)])
            second = dot_nn(att[...], w[:, pl.ds(pl.multiple_of(at + width, step), step)])
            for k in range(tp_count):
                rows_of = slice(k * each, (k + 1) * each)
                part[which, k, :, pl.ds(at, step)] = jnp.concatenate([first[rows_of], second[rows_of]], axis=0).astype(BF)
            return carry

        lax.fori_loop(0, width // step, columns, 0)

    def sum_copy(which, k):
        there = (tp + k) % tp_count
        return remote(part.at[which, there], got.at[which, k], p_send.at[which, k], p_recv.at[which, k], {"tp": there})

    def send_sums(which):
        for k in range(1, tp_count):
            sum_copy(which, k).start()

    def finish_sums(which, out_ref):
        each = tokens // tp_count
        total = part[which, tp].astype(F32)
        for k in range(1, tp_count):
            sum_copy(which, k).wait_recv()
            total = total + got[which, k].astype(F32)
        width = part.shape[3]
        out_ref[:, 0:width] = total[0:each].astype(BF)
        out_ref[:, width : 2 * width] = total[each : 2 * each].astype(BF)

    for item in loads:
        item.wait()

    ctx_count = 2 * ring
    span_total = ctx_count * tokens
    blocks = owner_ref.shape[1]
    per_dev = tokens // BLOCK
    token_at = lax.broadcasted_iota(jnp.int32, (blocks, span_total), 1)
    block_at = lax.broadcasted_iota(jnp.int32, (blocks, span_total), 0)
    ring_at = token_at // (2 * tokens)
    side_at = (token_at // tokens) % 2
    block_of = (side_at * ring + ring_at) * per_dev + (token_at % tokens) // BLOCK
    expand = jnp.where(block_of == block_at, 1.0, 0.0).astype(BF)
    other = 1 - pool
    owner_row = jnp.where(other == 0, owner_ref[0:1, :], owner_ref[1:2, :])
    slot_row = jnp.where(other == 0, slot_ref[0:1, :], slot_ref[1:2, :])
    owners = dot_nn(jnp.broadcast_to(owner_row, (8, blocks)).astype(F32).astype(BF), expand)[0:1, :]
    slots = dot_nn(jnp.broadcast_to(slot_row, (8, blocks)).astype(F32).astype(BF), expand)[0:1, :]
    slot_tokens = SLOTS * BLOCK
    place = lax.broadcasted_iota(jnp.int32, (slot_tokens, span_total), 0)
    source = lax.broadcasted_iota(jnp.int32, (slot_tokens, span_total), 1)
    chosen = (
        (owners == me.astype(F32))
        & (slots == (place // BLOCK).astype(F32))
        & (place % BLOCK == source % BLOCK)
    )
    picked = jnp.where(chosen, 1.0, 0.0).astype(BF)
    gath_k = gath[:, :, 0:tokens, :].reshape(span_total, HD)
    gath_v = gath[:, :, tokens : 2 * tokens, :].reshape(span_total, HD)
    slot_k = dot_nn(picked, gath_k).astype(BF)
    slot_v = dot_nn(picked, gath_v).astype(BF)
    filled = dot_nt(jnp.ones((8, span_total), BF), picked)[0:1, :]

    steps = 4
    group = BLOCK // steps
    cache = ck.shape[1]
    new_pad = jnp.zeros((HD - dk_ref.shape[0], HD), BF)
    dec_rows = HEADS_DEV * BLOCK
    row_id = lax.broadcasted_iota(jnp.int32, (dec_rows, HD), 0)
    col_id = lax.broadcasted_iota(jnp.int32, (dec_rows, HD), 1)
    crow_id = lax.broadcasted_iota(jnp.int32, (dec_rows, group * cache), 0)
    ccol_id = lax.broadcasted_iota(jnp.int32, (dec_rows, group * cache), 1)

    def decode_group(g, carry):
        at = pl.ds(pl.multiple_of(g * BLOCK, BLOCK), BLOCK)
        queries = split_query(
            jnp.concatenate([dq_ref[at, h * HD : (h + 1) * HD] for h in range(HEADS_DEV)], axis=0)
        )
        keys = jnp.concatenate(
            [ck[pl.ds(g * group, group)].reshape(group * cache, HD), slot_k, dk_ref[...], new_pad], axis=0
        )
        values = jnp.concatenate(
            [cv[pl.ds(g * group, group)].reshape(group * cache, HD), slot_v, dv_ref[...], new_pad], axis=0
        )
        scores = dot_nt(queries, jnp.concatenate([keys, keys], axis=1))
        live = jnp.zeros((dec_rows, group * cache), jnp.int32)
        for r in range(group):
            live = jnp.where(ccol_id // cache == r, len_ref[0, g * group + r], live)
        own_row = (crow_id % BLOCK) // steps == ccol_id // cache
        s_cache = jnp.where(own_row & (ccol_id % cache < live), scores[:, 0 : group * cache], NEG)
        s_slot = jnp.where(filled > 0.5, scores[:, group * cache : group * cache + slot_tokens], NEG)
        here = g * BLOCK + row_id % BLOCK
        see_new = (here // steps == col_id // steps) & (col_id % steps <= here % steps)
        s_new = jnp.where(see_new, scores[:, group * cache + slot_tokens :], NEG)
        masked = jnp.concatenate([s_cache, s_slot, s_new], axis=1)
        top = jnp.max(masked, axis=1, keepdims=True)
        weights = jnp.exp2(masked - top)
        total = jnp.sum(weights, axis=1, keepdims=True)
        out = (dot_nn(weights.astype(BF), values) / total).astype(BF)
        for h in range(HEADS_DEV):
            att[at, h * HD : (h + 1) * HD] = out[h * BLOCK : (h + 1) * BLOCK]
        return carry

    lax.fori_loop(0, dq_ref.shape[0] // BLOCK, decode_group, 0)
    project(1)
    send_sums(1)

    span_relay().wait_recv()
    for p in range(PIECES):
        piece_relay(p).wait_recv()
        at = pl.ds(piece_rows(p), chunk)
        if (p // 2) % 2 == 0:
            k_par[at, 0:HD] = par[p]
            k_par[at, HD : 2 * HD] = par[p]
        else:
            v_par[at, 0:HD] = par[p]
    for c in range(2):
        k_par[prompt : prompt + tokens, c * HD : (c + 1) * HD] = sk_ref[...]
        k_par[prompt + tokens : prompt + 2 * tokens, c * HD : (c + 1) * HD] = skv_par[0:tokens, :]
    v_par[prompt : prompt + tokens, 0:HD] = sv_ref[...]
    v_par[prompt + tokens : prompt + 2 * tokens, 0:HD] = skv_par[tokens : 2 * tokens, :]

    def out_copy(i):
        return remote(obuf.at[i], oin.at[i], o_send.at[i], o_recv.at[i], along_z(-way(i)))

    def stat_copy(i):
        return remote(sbuf.at[i], sin.at[i], st_send.at[i], st_recv.at[i], along_z(-way(i)))

    lane = lax.broadcasted_iota(jnp.int32, (8, HD), 1)
    groups = tokens // 8

    def merge(i, box):
        out_copy(box).wait_recv()
        stat_copy(box).wait_recv()
        stats = sin[box]
        for h in range(HEADS_DEV):
            for g in range(groups):
                at = slice(h * tokens + g * 8, h * tokens + g * 8 + 8)
                a = g * 16 + h
                in_m[at, :] = jnp.broadcast_to(stats[:, a : a + 1], (8, HD))
                in_l[at, :] = jnp.broadcast_to(stats[:, a + 8 : a + 9], (8, HD))
        top = jnp.maximum(mx[i], in_m[...])
        keep = jnp.exp2(mx[i] - top)
        add = jnp.exp2(in_m[...] - top)
        acc[i] = acc[i] * keep + oin[box].astype(F32) * add
        sm[i] = sm[i] * keep + in_l[...] * add
        mx[i] = top

    def pack(i):
        obuf[i] = acc[i].astype(BF)
        stats = jnp.zeros((8, HD), F32)
        for h in range(HEADS_DEV):
            for g in range(groups):
                at = pl.ds(h * tokens + g * 8, 8)
                a = g * 16 + h
                stats = jnp.where(lane == a, mx[i, at, :], stats)
                stats = jnp.where(lane == a + 8, sm[i, at, :], stats)
        sbuf[i] = stats

    def partner_step(n, carry):
        i = ring - 1 - n
        attend_partner(i)

        @pl.when(i + 2 < ring)
        def _():
            merge(i, i + 2)

        pack(i)
        out_copy(i).start()
        stat_copy(i).start()
        return carry

    lax.fori_loop(0, ring - 1, partner_step, 0)
    attend_partner(0)
    merge(0, 1)
    merge(0, 2)
    done = (acc[0] / sm[0]).astype(BF)
    for h in range(HEADS_DEV):
        att[:, h * HD : (h + 1) * HD] = done[h * tokens : (h + 1) * tokens]
    project(0)
    send_sums(0)
    finish_sums(1, dout_ref)
    finish_sums(0, pout_ref)

    query_copy(1, q_ref).wait_send()
    query_copy(2, q_ref).wait_send()
    for i in range(3, ring):
        query_copy(i, qall.at[i]).wait_send()
    for k in range(2):
        span_copy(k).wait_send()
    span_relay().wait_send()
    for i in range(1, ring):
        gather_copy(i, z).wait_send()
        out_copy(i).wait_send()
        stat_copy(i).wait_send()
    for p in range(PIECES):
        piece_copy(p).wait_send()
        piece_relay(p).wait_send()
    for which in range(2):
        for k in range(1, tp_count):
            sum_copy(which, k).wait_send()


def on_device(
    span_queries,
    span_keys,
    span_values,
    prompt_keys,
    prompt_values,
    block_owner,
    block_slot,
    decode_queries,
    decode_new_keys,
    decode_new_values,
    cache_keys,
    cache_values,
    cache_len,
    out_weight,
):
    ring = lax.axis_size("ctx") // 2
    tp_count = lax.axis_size("tp")
    tokens = span_queries.shape[1]
    width = span_queries.shape[2]
    prompt = prompt_keys.shape[1]
    row_count, step_count = decode_queries.shape[1:3]
    cache = cache_keys.shape[2]
    columns = out_weight.shape[1]
    rows = tokens * HEADS_DEV
    each = tokens // tp_count
    vmem = pl.BlockSpec(memory_space=pltpu.VMEM)
    smem = pl.BlockSpec(memory_space=pltpu.SMEM)
    anywhere = pl.BlockSpec(memory_space=pl.ANY)
    dma = pltpu.SemaphoreType.DMA
    prefill, decode = pl.pallas_call(
        lambda *refs: kernel(ring, tp_count, *refs),
        out_shape=(
            jax.ShapeDtypeStruct((each, columns), BF),
            jax.ShapeDtypeStruct((each, columns), BF),
        ),
        in_specs=[vmem] * 10 + [anywhere, anywhere, smem, anywhere],
        out_specs=(vmem, vmem),
        scratch_shapes=[
            pltpu.VMEM((ring, tokens, width), BF),
            pltpu.VMEM((2 * tokens, HD), BF),
            pltpu.VMEM((2 * tokens, HD), BF),
            pltpu.VMEM((ring, 2, 2 * tokens, HD), BF),
            pltpu.VMEM((PIECES, prompt // 4, HD), BF),
            pltpu.VMEM((PIECES, prompt // 4, HD), BF),
            pltpu.VMEM((prompt, 2 * HD), BF),
            pltpu.VMEM((prompt, 2 * HD), BF),
            pltpu.VMEM((prompt + 2 * tokens, 2 * HD), BF),
            pltpu.VMEM((prompt + 2 * tokens, 2 * HD), BF),
            pltpu.VMEM((ring, rows, HD), F32),
            pltpu.VMEM((ring, rows, HD), F32),
            pltpu.VMEM((ring, rows, HD), F32),
            pltpu.VMEM((rows, HD), F32),
            pltpu.VMEM((rows, HD), F32),
            pltpu.VMEM((ring, rows, HD), BF),
            pltpu.VMEM((ring, 8, HD), F32),
            pltpu.VMEM((ring, rows, HD), BF),
            pltpu.VMEM((ring, 8, HD), F32),
            pltpu.VMEM((width, columns), BF),
            pltpu.VMEM((row_count, cache, HD), BF),
            pltpu.VMEM((row_count, cache, HD), BF),
            pltpu.VMEM((tokens, width), BF),
            pltpu.VMEM((2, tp_count, 2 * each, columns // 2), BF),
            pltpu.VMEM((2, tp_count, 2 * each, columns // 2), BF),
            dma((ring,)),
            dma((ring,)),
            dma((2,)),
            dma((2,)),
            dma((1,)),
            dma((1,)),
            dma((ring,)),
            dma((ring,)),
            dma((PIECES,)),
            dma((PIECES,)),
            dma((PIECES,)),
            dma((PIECES,)),
            dma((ring,)),
            dma((ring,)),
            dma((ring,)),
            dma((ring,)),
            dma((2, tp_count)),
            dma((2, tp_count)),
            dma((3,)),
        ],
        compiler_params=pltpu.CompilerParams(
            collective_id=0, has_side_effects=True, vmem_limit_bytes=60 * 1024 * 1024
        ),
        name="serve",
    )(
        span_queries[0],
        span_keys[0],
        span_values[0],
        prompt_keys[0],
        prompt_values[0],
        block_owner,
        block_slot,
        decode_queries.reshape(row_count * step_count, width),
        decode_new_keys.reshape(row_count * step_count, HD),
        decode_new_values.reshape(row_count * step_count, HD),
        cache_keys[0],
        cache_values[0],
        cache_len,
        out_weight,
    )
    return (prefill[None], decode.reshape(1, row_count // tp_count, step_count, columns))


def solution(mesh):
    in_specs = (
        P("grp", "ctx", "tp"),
        P("grp", "ctx", "tp"),
        P("grp", "ctx", "tp"),
        P("grp", "ctx", "tp"),
        P("grp", "ctx", "tp"),
        P(),
        P(),
        P("grp", "ctx", None, "tp"),
        P("grp", "ctx", None, "tp"),
        P("grp", "ctx", None, "tp"),
        P("grp", "ctx", None, "tp"),
        P("grp", "ctx", None, "tp"),
        P("grp", "ctx"),
        P("tp", None),
    )
    out_specs = (P("grp", ("ctx", "tp"), None), P("grp", ("ctx", "tp"), None, None))
    return jax.shard_map(
        on_device, mesh=mesh, in_specs=in_specs, out_specs=out_specs, check_vma=False
    )
```

time: 459 us -> 76.6 us (0.17)
  blocking collectives: 142 us -> 0 us
  waiting for transfers between devices: 131 us -> 0 us
  matrix products: 92.9 us -> 0 us
  Pallas kernels: 0 us -> 71.2 us
  other arithmetic: 30 us -> 0 us
  local copies, waits for them, and re-layouts: 29.6 us -> 4.56 us
  between operations: 15.7 us -> 0.64 us
  loops' own time: 11.5 us -> 0 us
    all_gather x4 -> x0, blocking collectives: 142 us -> none  [the longest x1 38.8 us: on_device(): lax.all_gather(span_k, 'ctx', axis=0, tiled=True)]
    all_gather x2 -> x0, waiting for transfers between devices: 103 us -> none  [the longest x1 103 us: on_device(): lax.all_gather(prompt_v, 'ctx', axis=0, tiled=True)]
    dot_general x44 -> x0, matrix products: 92.9 us -> none  [the longest x17 36.9 us: advance(): jnp.einsum('tkgs,skd->tkgd', weights.astype(jnp.bfloat16), block_values,...]
    pallas_call x0 -> x1, Pallas kernels: none -> 71.2 us  [on_device(): pl.pallas_call(lambda *refs: kernel(ring, tp_count, *refs), out_shape=(ja...]
    reduce_scatter x2 -> x0, waiting for transfers between devices: 26.9 us -> none  [on_device(): lax.psum_scatter(jnp.dot(row_block, out_weight, preferred_element_type=jn...]
    reduce_sum x20 -> x0, other arithmetic: 24.7 us -> none  [the longest x17 21.1 us: advance(): weight_sum = weight_sum * rescale + jnp.sum(weights, axis=-1)]
    another operation x1 -> x0, loops' own time: 11.5 us -> none  [attend_block(): lax.scan(advance, softmax_state, (key_blocks, value_blocks, jnp.arange(bl...]
    while x80 -> x0, local copies, waits for them, and re-layouts: 10.9 us -> none
  transfers between devices with their start and end apart: 6 -> 0, of which waited for: 2 -> 0; matrix products, arithmetic and copies ran while one was open for 31% -> 0% of each run, Pallas kernels for 0% -> 0%
where the time goes in v1:
time: 76.6 us; the launch traced here: 76.4 us
  Pallas kernels  71.2 us (93%)
  local copies, waits for them, and re-layouts  4.56 us (6%)
    pallas_call x1, Pallas kernels, on_device(): pl.pallas_call(lambda *refs: kernel(ring, tp_count, *refs), out_shape=(ja...  71.2 us
    reshape x1, local copies, waits for them, and re-layouts, on_device(): decode_queries.reshape(row_count * step_count, width)  1.59 us

profile of v1, /device:TPU:1, one launch (start us, length us, event | category | flops | bytes accessed | tf_op | source)
XLA Modules:
  0.0 76.4 jit_solution(16613028141990651442)
XLA Ops:
  0.6 1.6 %reshape.16.refs_7_ = bf16[64,1024]{1,0:T(8,128)(2,1)} reshape(bf16[1,16,4,1024]{3,2,1,0:T(4,128)(2,1)} %param.21) | data formatting | bytes 262144 | tf_op jit(solution)/shard_map/reshape | solution.py:506
  2.2 71.2 %serve.1 = (bf16[8,4096]{1,0:T(8,128)(2,1)}, bf16[8,4096]{1,0:T(8,128)(2,1)}) custom-call(bf16[64,1024]{1,0:T(8,128)(2,1)} %bitcast.14, bf16[64,128]{1,0:T(8,128)(2,1)} %bitcast.16, bf16[64,128]{1,0:T(8,128)(2,1)} %bitcast.17, bf16[2048,128]{1,0:T(8,128)(2,1)} %bitcast.12, bf16[2048,128]{1,0:T(8,128)(2,1)} %bitcast.13, s32[2,64]{1,0:T(2,128)} %refs_5_.1, ...), custom_call_target="tpu_custom_call" | custom-call | tf_op jit(solution)/shard_map/serve/pallas_call | solution.py:440
  73.4 1.5 %reshape.19 = bf16[1,2,4,4096]{3,2,1,0:T(4,128)(2,1)} reshape(bf16[8,4096]{1,0:T(8,128)(2,1)} %get-tuple-element.5) | data formatting | bytes 131072 | tf_op jit(solution)/shard_map/reshape | solution.py:514
  74.9 1.5 %copy.17 = bf16[1,8,4096]{2,1,0:T(8,128)(2,1)} copy(bf16[1,8,4096]{2,1,0:T(8,128)(2,1)} %bitcast.15) | data formatting | bytes 131072

commit v2 on v1

v2 whole, which is shorter than its diff:
```python
import math

import jax
import jax.numpy as jnp
from jax import lax
from jax.experimental import pallas as pl
from jax.experimental.pallas import tpu as pltpu
from jax.sharding import PartitionSpec as P

HD = 128
BLOCK = 16
SLOTS = 8
HEADS_DEV = 8
PIECES = 8
NEG = -1e30
SCALE2 = HD**-0.5 * math.log2(math.e)
MESH = pl.DeviceIdType.MESH
BF = jnp.bfloat16
F32 = jnp.float32


def dot_nt(a, b):
    return lax.dot_general(a, b, (((1,), (1,)), ((), ())), preferred_element_type=F32)


def dot_nn(a, b):
    return jnp.dot(a, b, preferred_element_type=F32)


def split_query(q):
    scaled = q.astype(F32) * SCALE2
    high = scaled.astype(BF)
    low = (scaled - high.astype(F32)).astype(BF)
    return jnp.concatenate([high, low], axis=1)


def kernel(
    ring, tp_count,
    q_ref, sk_ref, sv_ref, pk_ref, pv_ref, owner_ref, slot_ref, dq_ref, dk_ref, dv_ref, ck_hbm, cv_hbm, len_ref, w_hbm,
    out_ref,
    qbuf, skv, skv_par, gath, rel, par, k_raw, k_own, v_own, k_first, v_first, k_last, v_last,
    acc, mx, sm, in_m, in_l, obuf, sbuf, oin, sin,
    w, ck, cv, att, part, got,
    q_send, q_recv, s_send, s_recv, sp_send, sp_recv, g_send, g_recv, r_send, r_recv, f_send, f_recv,
    o_send, o_recv, st_send, st_recv, p_send, p_recv, load,
):
    me = lax.axis_index("ctx")
    pool = lax.axis_index("grp")
    tp = lax.axis_index("tp")
    y_hi = me // ring
    z = me % ring
    y = y_hi * 2 + pool
    far = ring // 2
    tokens = sk_ref.shape[0]
    prompt = pk_ref.shape[0]
    chunk = prompt // 4
    half_heads = HEADS_DEV // 2
    half_width = half_heads * HD
    half = tokens * half_heads

    def along_z(step):
        return {"ctx": y_hi * ring + (z + step + ring) % ring}

    def along_y(step):
        there = (y + step + 4) % 4
        return {"ctx": (there // 2) * ring + z, "grp": there % 2}

    def remote(src, dst, send, recv, device):
        return pltpu.make_async_remote_copy(
            src_ref=src, dst_ref=dst, send_sem=send, recv_sem=recv, device_id=device, device_id_type=MESH
        )

    def away(u):
        return 1 - 2 * ((u % 4) // 2)

    def source_z(u):
        return (z - away(u) * (u // 4) + 2 * ring) % ring

    def goes_on(u):
        d, r = u // 4, u % 4
        return jnp.logical_or(d + 1 < far, jnp.logical_and(d + 1 == far, r * (r - 3) == 0))

    def pair(n):
        first = 4 * ((n + 1) // 2) + 2 * ((n + 1) % 2) * ((n + ring - 2) // (ring - 1))
        return first, first + 1 + 2 * (n // (ring - 1))

    sent = [u for u in range(4, 4 * far + 4) if u // 4 < far or u % 4 in (0, 3)]

    def query_copy(u, src):
        return remote(src, qbuf.at[u], q_send.at[u], q_recv.at[u], along_z(away(u)))

    def span_copy(k):
        return remote(skv, gath.at[z, y_hi], s_send.at[k], s_recv.at[k], along_y(1 - 2 * k))

    def span_relay():
        return remote(gath.at[z, ((y + 3) % 4) // 2], skv_par, sp_send.at[0], sp_recv.at[0], along_y(1))

    def gather_copy(i, at):
        return remote(gath.at[at], gath.at[at], g_send.at[i], g_recv.at[i], along_z(2 * (i % 2) - 1))

    def gather_z(i):
        return (z - (2 * (i % 2) - 1) * ((i + 1) // 2) + ring) % ring

    def piece_copy(p):
        src = (pk_ref if (p // 2) % 2 == 0 else pv_ref).at[pl.ds(((p % 2) * 2 + p // 4) * chunk, chunk)]
        return remote(src, rel.at[p], r_send.at[p], r_recv.at[p], along_y(1 - 2 * (p % 2)))

    def piece_relay(p):
        return remote(rel.at[p], par.at[p], f_send.at[p], f_recv.at[p], along_y(1 - 2 * (p % 2)))

    def forward_piece(p):
        remote(rel.at[p], rel.at[p], r_send.at[p], r_recv.at[p], along_y(1)).wait_recv()
        piece_relay(p).start()

    def own_half(b):
        return q_ref.at[:, pl.ds(b * half_width, half_width)]

    loads = [
        pltpu.make_async_copy(pk_ref, k_raw, load.at[0]),
        pltpu.make_async_copy(pv_ref, v_own.at[:, pl.ds(0, HD)], load.at[1]),
        pltpu.make_async_copy(own_half(0), qbuf.at[0], load.at[2]),
        pltpu.make_async_copy(own_half(1), qbuf.at[1], load.at[3]),
        pltpu.make_async_copy(ck_hbm, ck, load.at[4]),
        pltpu.make_async_copy(cv_hbm, cv, load.at[5]),
        pltpu.make_async_copy(w_hbm, w, load.at[6]),
    ]
    for item in loads[:4]:
        item.start()

    barrier = pltpu.get_barrier_semaphore()
    for device in (along_z(1), along_z(-1), along_y(1), along_y(-1)):
        pl.semaphore_signal(barrier, inc=1, device_id=device, device_id_type=MESH)
    for k in range(1, tp_count):
        pl.semaphore_signal(barrier, inc=1, device_id={"tp": (tp + k) % tp_count}, device_id_type=MESH)
    skv[0:tokens, :] = sk_ref[...]
    skv[tokens : 2 * tokens, :] = sv_ref[...]
    pl.semaphore_wait(barrier, 4 + tp_count - 1)

    for u in range(4, 8):
        query_copy(u, own_half(u % 2)).start()
    span_copy(0).start()
    span_copy(1).start()
    for p in range(PIECES):
        piece_copy(p).start()
    for item in loads[4:]:
        item.start()

    v_own[:, HD : 2 * HD] = jnp.ones((prompt, HD), BF)
    v_first[:, HD : 2 * HD] = jnp.ones((v_first.shape[0], HD), BF)
    v_last[:, HD : 2 * HD] = jnp.ones((v_last.shape[0], HD), BF)
    for item in loads[:4]:
        item.wait()

    def put_keys(dst, at, rows):
        turned = rows.T
        size = rows.shape[0]
        dst[0:HD, at : at + size] = turned
        dst[HD : 2 * HD, at : at + size] = turned

    for c in range(4):
        put_keys(k_own, c * chunk, k_raw[c * chunk : (c + 1) * chunk])

    def queries_of(u):
        parts = [qbuf[u, :, h * HD : (h + 1) * HD] for h in range(half_heads)]
        return split_query(jnp.concatenate(parts, axis=0))

    def attend(u, keys, values, fresh, span):
        scores = dot_nn(queries_of(u), keys[...])
        if span:
            query_ctx = y_hi * ring + source_z(u)
            partner = (1 - y_hi) * ring + z
            token = lax.broadcasted_iota(jnp.int32, (half, 2 * tokens), 0) % tokens
            key = lax.broadcasted_iota(jnp.int32, (half, 2 * tokens), 1)
            key_pos = jnp.where(key < tokens, me * tokens + key, partner * tokens + key - tokens)
            seen = jnp.where(key_pos <= query_ctx * tokens + token, scores[:, prompt // 2 :], NEG)
            scores = jnp.concatenate([scores[:, 0 : prompt // 2], seen], axis=1)
        top = jnp.max(scores, axis=1, keepdims=True)
        if not fresh:
            before = mx[u, :, 0:1]
            top = jnp.maximum(top, before)
        out = dot_nn(jnp.exp2(scores - top).astype(BF), values[...])
        if fresh:
            acc[u] = out[:, 0:HD]
            sm[u] = out[:, HD : 2 * HD]
        else:
            keep = jnp.exp2(before - top)
            acc[u] = acc[u] * keep + out[:, 0:HD]
            sm[u] = sm[u] * keep + out[:, HD : 2 * HD]
        mx[u] = jnp.broadcast_to(top, (half, HD))

    def own_step(n, carry):
        halves = pair(n)

        @pl.when(n > 0)
        def _():
            for u in halves:
                query_copy(u, qbuf.at[u]).wait_recv()

                @pl.when(goes_on(u))
                def _():
                    query_copy(u + 4, qbuf.at[u]).start()

        for u in halves:
            attend(u, k_own, v_own, True, False)

        @pl.when(n == 0)
        def _():
            for k in range(2):
                span_copy(k).wait_recv()
            span_relay().start()
            gather_copy(1, z).start()
            gather_copy(2, z).start()

        @pl.when(n > 0)
        def _():
            forward_piece(n - 1)
            at = gather_z(n)
            gather_copy(n, at).wait_recv()

            @pl.when(n + 2 < ring)
            def _():
                gather_copy(n + 2, at).start()

        return carry

    lax.fori_loop(0, ring, own_step, 0)
    for p in range(ring - 1, PIECES):
        forward_piece(p)

    each = tokens // tp_count
    step = part.shape[4]
    width = w.shape[1] // 2

    def sum_copy(which, j, k):
        there = (tp + k) % tp_count
        return remote(
            part.at[which, j, there], got.at[which, j, k], p_send.at[which, j, k], p_recv.at[which, j, k], {"tp": there}
        )

    def project(which):
        def columns(j, carry):
            at = pl.multiple_of(j * step, step)
            first = dot_nn(att[...], w[:, pl.ds(at, step)])
            second = dot_nn(att[...], w[:, pl.ds(pl.multiple_of(at + width, step), step)])
            for k in range(tp_count):
                rows_of = slice(k * each, (k + 1) * each)
                part[which, j, k] = jnp.concatenate([first[rows_of], second[rows_of]], axis=0).astype(BF)
            for k in range(1, tp_count):
                sum_copy(which, j, k).start()
            return carry

        lax.fori_loop(0, width // step, columns, 0)

    def summed(which, j):
        total = part[which, j, tp].astype(F32)
        for k in range(1, tp_count):
            sum_copy(which, j, k).wait_recv()
            total = total + got[which, j, k].astype(F32)
        return total

    for item in loads[4:]:
        item.wait()

    ctx_count = 2 * ring
    span_total = ctx_count * tokens
    blocks = owner_ref.shape[1]
    per_dev = tokens // BLOCK
    token_at = lax.broadcasted_iota(jnp.int32, (blocks, span_total), 1)
    block_at = lax.broadcasted_iota(jnp.int32, (blocks, span_total), 0)
    ring_at = token_at // (2 * tokens)
    side_at = (token_at // tokens) % 2
    block_of = (side_at * ring + ring_at) * per_dev + (token_at % tokens) // BLOCK
    expand = jnp.where(block_of == block_at, 1.0, 0.0).astype(BF)
    other = 1 - pool
    owner_row = jnp.where(other == 0, owner_ref[0:1, :], owner_ref[1:2, :])
    slot_row = jnp.where(other == 0, slot_ref[0:1, :], slot_ref[1:2, :])
    owners = dot_nn(jnp.broadcast_to(owner_row, (8, blocks)).astype(F32).astype(BF), expand)[0:1, :]
    slots = dot_nn(jnp.broadcast_to(slot_row, (8, blocks)).astype(F32).astype(BF), expand)[0:1, :]
    slot_tokens = SLOTS * BLOCK
    place = lax.broadcasted_iota(jnp.int32, (slot_tokens, span_total), 0)
    source = lax.broadcasted_iota(jnp.int32, (slot_tokens, span_total), 1)
    chosen = (
        (owners == me.astype(F32))
        & (slots == (place // BLOCK).astype(F32))
        & (place % BLOCK == source % BLOCK)
    )
    picked = jnp.where(chosen, 1.0, 0.0).astype(BF)
    gath_k = gath[:, :, 0:tokens, :].reshape(span_total, HD)
    gath_v = gath[:, :, tokens : 2 * tokens, :].reshape(span_total, HD)
    slot_k = dot_nn(picked, gath_k).astype(BF)
    slot_v = dot_nn(picked, gath_v).astype(BF)
    filled = dot_nt(jnp.ones((8, span_total), BF), picked)[0:1, :]

    steps = 4
    group = BLOCK // steps
    cache = ck.shape[1]
    new_pad = jnp.zeros((HD - dk_ref.shape[0], HD), BF)
    dec_rows = HEADS_DEV * BLOCK
    row_id = lax.broadcasted_iota(jnp.int32, (dec_rows, HD), 0)
    col_id = lax.broadcasted_iota(jnp.int32, (dec_rows, HD), 1)
    crow_id = lax.broadcasted_iota(jnp.int32, (dec_rows, group * cache), 0)
    ccol_id = lax.broadcasted_iota(jnp.int32, (dec_rows, group * cache), 1)

    def decode_group(g, carry):
        at = pl.ds(pl.multiple_of(g * BLOCK, BLOCK), BLOCK)
        asked = dq_ref[pl.ds(g * group, group)].astype(F32).reshape(BLOCK, HEADS_DEV * HD)
        queries = jnp.concatenate([asked[:, h * HD : (h + 1) * HD] for h in range(HEADS_DEV)], axis=0).astype(BF)
        keys = jnp.concatenate(
            [ck[pl.ds(g * group, group)].reshape(group * cache, HD), slot_k, dk_ref[...], new_pad], axis=0
        )
        values = jnp.concatenate(
            [cv[pl.ds(g * group, group)].reshape(group * cache, HD), slot_v, dv_ref[...], new_pad], axis=0
        )
        scores = dot_nt(queries, keys) * SCALE2
        live = jnp.zeros((dec_rows, group * cache), jnp.int32)
        for r in range(group):
            live = jnp.where(ccol_id // cache == r, len_ref[0, g * group + r], live)
        own_row = (crow_id % BLOCK) // steps == ccol_id // cache
        s_cache = jnp.where(own_row & (ccol_id % cache < live), scores[:, 0 : group * cache], NEG)
        s_slot = jnp.where(filled > 0.5, scores[:, group * cache : group * cache + slot_tokens], NEG)
        here = g * BLOCK + row_id % BLOCK
        see_new = (here // steps == col_id // steps) & (col_id % steps <= here % steps)
        s_new = jnp.where(see_new, scores[:, group * cache + slot_tokens :], NEG)
        masked = jnp.concatenate([s_cache, s_slot, s_new], axis=1)
        top = jnp.max(masked, axis=1, keepdims=True)
        weights = jnp.exp2(masked - top)
        total = jnp.sum(weights, axis=1, keepdims=True)
        out = (dot_nn(weights.astype(BF), values) / total).astype(BF)
        for h in range(HEADS_DEV):
            att[at, h * HD : (h + 1) * HD] = out[h * BLOCK : (h + 1) * BLOCK]
        return carry

    lax.fori_loop(0, dq_ref.shape[0] // group, decode_group, 0)
    project(1)

    def place_piece(p, keys, values):
        piece_relay(p).wait_recv()
        at = (p % 2) * chunk
        if (p // 2) % 2 == 0:
            put_keys(keys, at, par[p])
        else:
            values[at : at + chunk, 0:HD] = par[p]

    for p in range(4):
        place_piece(p, k_first, v_first)

    def first_step(n, carry):
        for u in pair(n):
            attend(u, k_first, v_first, False, False)
        return carry

    lax.fori_loop(0, ring, first_step, 0)

    span_relay().wait_recv()
    put_keys(k_last, 2 * chunk, jnp.concatenate([sk_ref[...], skv_par[0:tokens, :]], axis=0))
    v_last[2 * chunk : 2 * chunk + tokens, 0:HD] = sv_ref[...]
    v_last[2 * chunk + tokens : 2 * chunk + 2 * tokens, 0:HD] = skv_par[tokens : 2 * tokens, :]
    for p in range(4, 8):
        place_piece(p, k_last, v_last)

    def out_copy(u):
        return remote(obuf.at[u], oin.at[u], o_send.at[u], o_recv.at[u], along_z(-away(u)))

    def stat_copy(u):
        return remote(sbuf.at[u], sin.at[u], st_send.at[u], st_recv.at[u], along_z(-away(u)))

    lane = lax.broadcasted_iota(jnp.int32, (8, HD), 1)

    def merge(u, box):
        out_copy(box).wait_recv()
        stat_copy(box).wait_recv()
        stats = sin[box]
        for a in range(half // 8):
            in_m[8 * a : 8 * a + 8, :] = jnp.broadcast_to(stats[:, a : a + 1], (8, HD))
            in_l[8 * a : 8 * a + 8, :] = jnp.broadcast_to(stats[:, a + 64 : a + 65], (8, HD))
        top = jnp.maximum(mx[u], in_m[...])
        keep = jnp.exp2(mx[u] - top)
        add = jnp.exp2(in_m[...] - top)
        acc[u] = acc[u] * keep + oin[box].astype(F32) * add
        sm[u] = sm[u] * keep + in_l[...] * add
        mx[u] = top

    def pack(u):
        obuf[u] = acc[u].astype(BF)
        stats = jnp.zeros((8, HD), F32)
        for a in range(half // 8):
            at = pl.ds(8 * a, 8)
            stats = jnp.where(lane == a, mx[u, at, :], stats)
            stats = jnp.where(lane == a + 64, sm[u, at, :], stats)
        sbuf[u] = stats

    def last_step(m, carry):
        n = ring - 1 - m
        halves = pair(n)
        for u in halves:
            attend(u, k_last, v_last, False, True)
        for u in halves:
            @pl.when(goes_on(u))
            def _():
                merge(u, u + 4)

            pack(u)
            out_copy(u).start()
            stat_copy(u).start()
        return carry

    lax.fori_loop(0, ring - 1, last_step, 0)
    for u in range(2):
        attend(u, k_last, v_last, False, True)
    for u in range(2):
        merge(u, u + 4)
        merge(u, u + 6)
        done = (acc[u] / sm[u]).astype(BF)
        for h in range(half_heads):
            column = (u * half_heads + h) * HD
            att[:, column : column + HD] = done[h * tokens : (h + 1) * tokens]
    project(0)
    for j in range(width // step):
        decode_sum = summed(1, j)
        prefill_sum = summed(0, j)
        for c in range(2):
            rows_of = slice(c * each, (c + 1) * each)
            both = jnp.concatenate([prefill_sum[rows_of], decode_sum[rows_of]], axis=0).astype(BF)
            out_ref[:, c * width + j * step : c * width + (j + 1) * step] = both

    for u in sent:
        query_copy(u, qbuf.at[u]).wait_send()
        out_copy(u).wait_send()
        stat_copy(u).wait_send()
    for k in range(2):
        span_copy(k).wait_send()
    span_relay().wait_send()
    for i in range(1, ring):
        gather_copy(i, z).wait_send()
    for p in range(PIECES):
        piece_copy(p).wait_send()
        piece_relay(p).wait_send()
    for which in range(2):
        for j in range(width // step):
            for k in range(1, tp_count):
                sum_copy(which, j, k).wait_send()


def separate(sums_ref, prefill_ref, decode_ref):
    each = prefill_ref.shape[0]
    sums = sums_ref[...].astype(F32)
    prefill_ref[...] = sums[0:each].astype(BF)
    steps = decode_ref.shape[1]
    for r in range(decode_ref.shape[0]):
        decode_ref[r] = sums[each + r * steps : each + (r + 1) * steps].astype(BF)


def on_device(
    span_queries,
    span_keys,
    span_values,
    prompt_keys,
    prompt_values,
    block_owner,
    block_slot,
    decode_queries,
    decode_new_keys,
    decode_new_values,
    cache_keys,
    cache_values,
    cache_len,
    out_weight,
):
    ring = lax.axis_size("ctx") // 2
    tp_count = lax.axis_size("tp")
    tokens = span_queries.shape[1]
    width = span_queries.shape[2]
    prompt = prompt_keys.shape[1]
    row_count, step_count = decode_queries.shape[1:3]
    cache = cache_keys.shape[2]
    columns = out_weight.shape[1]
    each = tokens // tp_count
    count = 4 * (ring // 2) + 4
    half = tokens * HEADS_DEV // 2
    step = min(512, columns // 2)
    blocks = columns // 2 // step
    span = 2 * tokens
    vmem = pl.BlockSpec(memory_space=pltpu.VMEM)
    smem = pl.BlockSpec(memory_space=pltpu.SMEM)
    anywhere = pl.BlockSpec(memory_space=pl.ANY)
    dma = pltpu.SemaphoreType.DMA
    sums = pl.pallas_call(
        lambda *refs: kernel(ring, tp_count, *refs),
        out_shape=jax.ShapeDtypeStruct((2 * each, columns), BF),
        in_specs=[anywhere, vmem, vmem, anywhere, anywhere] + [vmem] * 5 + [anywhere, anywhere, smem, anywhere],
        out_specs=vmem,
        scratch_shapes=[
            pltpu.VMEM((count, tokens, width // 2), BF),
            pltpu.VMEM((span, HD), BF),
            pltpu.VMEM((span, HD), BF),
            pltpu.VMEM((ring, 2, span, HD), BF),
            pltpu.VMEM((PIECES, prompt // 4, HD), BF),
            pltpu.VMEM((PIECES, prompt // 4, HD), BF),
            pltpu.VMEM((prompt, HD), BF),
            pltpu.VMEM((2 * HD, prompt), BF),
            pltpu.VMEM((prompt, 2 * HD), BF),
            pltpu.VMEM((2 * HD, prompt // 2), BF),
            pltpu.VMEM((prompt // 2, 2 * HD), BF),
            pltpu.VMEM((2 * HD, prompt // 2 + span), BF),
            pltpu.VMEM((prompt // 2 + span, 2 * HD), BF),
            pltpu.VMEM((count, half, HD), F32),
            pltpu.VMEM((count, half, HD), F32),
            pltpu.VMEM((count, half, HD), F32),
            pltpu.VMEM((half, HD), F32),
            pltpu.VMEM((half, HD), F32),
            pltpu.VMEM((count, half, HD), BF),
            pltpu.VMEM((count, 8, HD), F32),
            pltpu.VMEM((count, half, HD), BF),
            pltpu.VMEM((count, 8, HD), F32),
            pltpu.VMEM((width, columns), BF),
            pltpu.VMEM((row_count, cache, HD), BF),
            pltpu.VMEM((row_count, cache, HD), BF),
            pltpu.VMEM((tokens, width), BF),
            pltpu.VMEM((2, blocks, tp_count, 2 * each, step), BF),
            pltpu.VMEM((2, blocks, tp_count, 2 * each, step), BF),
            dma((count,)),
            dma((count,)),
            dma((2,)),
            dma((2,)),
            dma((1,)),
            dma((1,)),
            dma((ring,)),
            dma((ring,)),
            dma((PIECES,)),
            dma((PIECES,)),
            dma((PIECES,)),
            dma((PIECES,)),
            dma((count,)),
            dma((count,)),
            dma((count,)),
            dma((count,)),
            dma((2, blocks, tp_count)),
            dma((2, blocks, tp_count)),
            dma((7,)),
        ],
        compiler_params=pltpu.CompilerParams(
            collective_id=0, has_side_effects=True, vmem_limit_bytes=60 * 1024 * 1024
        ),
        name="serve",
    )(
        span_queries[0],
        span_keys[0],
        span_values[0],
        prompt_keys[0],
        prompt_values[0],
        block_owner,
        block_slot,
        decode_queries[0],
        decode_new_keys.reshape(row_count * step_count, HD),
        decode_new_values.reshape(row_count * step_count, HD),
        cache_keys[0],
        cache_values[0],
        cache_len,
        out_weight,
    )
    prefill, decode = pl.pallas_call(
        separate,
        out_shape=(
            jax.ShapeDtypeStruct((each, columns), BF),
            jax.ShapeDtypeStruct((row_count // tp_count, step_count, columns), BF),
        ),
        in_specs=[vmem],
        out_specs=(vmem, vmem),
        name="separate",
    )(sums)
    return (prefill[None], decode[None])


def solution(mesh):
    in_specs = (
        P("grp", "ctx", "tp"),
        P("grp", "ctx", "tp"),
        P("grp", "ctx", "tp"),
        P("grp", "ctx", "tp"),
        P("grp", "ctx", "tp"),
        P(),
        P(),
        P("grp", "ctx", None, "tp"),
        P("grp", "ctx", None, "tp"),
        P("grp", "ctx", None, "tp"),
        P("grp", "ctx", None, "tp"),
        P("grp", "ctx", None, "tp"),
        P("grp", "ctx"),
        P("tp", None),
    )
    out_specs = (P("grp", ("ctx", "tp"), None), P("grp", ("ctx", "tp"), None, None))
    return jax.shard_map(
        on_device, mesh=mesh, in_specs=in_specs, out_specs=out_specs, check_vma=False
    )
```

time: 76.6 us -> 82.8 us (1.081)
  Pallas kernels: 71.2 us -> 82.1 us
  local copies, waits for them, and re-layouts: 4.56 us -> 0 us
    pallas_call x1 -> x2, Pallas kernels: 71.2 us -> 82.1 us  [the longest x1 80.5 us: on_device(): pl.pallas_call(lambda *refs: kernel(ring, tp_count, *refs), out_shape=jax...]
    reshape x2 -> x0, local copies, waits for them, and re-layouts: 3.09 us -> none  [the longest x1 1.59 us: on_device(): decode_queries.reshape(row_count * step_count, width)]
    unnamed x1 -> x0, local copies, waits for them, and re-layouts: 1.47 us -> none
where the time goes in v2:
time: 82.8 us; the launch traced here: 82.7 us
  Pallas kernels  82.1 us (99%)
    pallas_call x1, Pallas kernels, on_device(): pl.pallas_call(lambda *refs: kernel(ring, tp_count, *refs), out_shape=jax...  80.5 us

profile of v2, /device:TPU:1, one launch (start us, length us, event | category | flops | bytes accessed | tf_op | source)
XLA Modules:
  0.0 82.7 jit_solution(17171765992902944182)
XLA Ops:
  0.6 80.5 %serve.1.sums_ref = bf16[16,4096]{1,0:T(8,128)(2,1)} custom-call(bf16[64,1024]{1,0:T(8,128)(2,1)} %bitcast.16, bf16[64,128]{1,0:T(8,128)(2,1)} %bitcast.18, bf16[64,128]{1,0:T(8,128)(2,1)} %bitcast.19, bf16[2048,128]{1,0:T(8,128)(2,1)} %bitcast.14, bf16[2048,128]{1,0:T(8,128)(2,1)} %bitcast.15, s32[2,64]{1,0:T(2,128)} %refs_5_.1, s32[2,64]{1,0:T(2,128)} %refs_6_.1, ...), custom_call_target="tpu_custom_call" | custom-call | tf_op jit(solution)/shard_map/serve/pallas_call | solution.py:487
  81.1 1.6 %separate.1 = (bf16[8,4096]{1,0:T(8,128)(2,1)}, bf16[2,4,4096]{2,1,0:T(4,128)(2,1)}) custom-call(bf16[16,4096]{1,0:T(8,128)(2,1)} %serve.1.sums_ref), custom_call_target="tpu_custom_call" | custom-call | tf_op jit(solution)/shard_map/separate/pallas_call | solution.py:561

commit v3 on v2

v3 whole, which is shorter than its diff:
```python
import math

import jax
import jax.numpy as jnp
from jax import lax
from jax.experimental import pallas as pl
from jax.experimental.pallas import tpu as pltpu
from jax.sharding import PartitionSpec as P

HD = 128
BLOCK = 16
SLOTS = 8
HEADS_DEV = 8
PIECES = 4
TILE = 256
NEG = -1e30
SCALE2 = HD**-0.5 * math.log2(math.e)
MESH = pl.DeviceIdType.MESH
BF = jnp.bfloat16
F32 = jnp.float32


def dot_nt(a, b):
    return lax.dot_general(a, b, (((1,), (1,)), ((), ())), preferred_element_type=F32)


def dot_nn(a, b):
    return jnp.dot(a, b, preferred_element_type=F32)


def split_query(q):
    scaled = q.astype(F32) * SCALE2
    high = scaled.astype(BF)
    low = (scaled - high.astype(F32)).astype(BF)
    return jnp.concatenate([high, low], axis=1)


def low_bits(x, size):
    return jnp.bitwise_and(x, size - 1)


def high_bits(x, size):
    return lax.shift_right_logical(x, size.bit_length() - 1)


def kernel(
    ring, tp_count,
    q_ref, sk_ref, sv_ref, pk_ref, pv_ref, owner_ref, slot_ref, dq_ref, dk_ref, dv_ref, ck_hbm, cv_hbm, len_ref, w_hbm,
    out_ref,
    qbuf, skv, skv_par, gath, rel, par, k_raw, k_own, v_own, k_par, v_par, scores, weights,
    acc, mx, sm, in_m, in_l, obuf, oin,
    w, ck, cv, att, part, sib, pairs, got,
    q_send, q_recv, s_send, s_recv, sp_send, sp_recv, g_send, g_recv, r_send, r_recv, f_send, f_recv,
    o_send, o_recv, c_send, c_recv, p_send, p_recv, load,
):
    me = lax.axis_index("ctx")
    pool = lax.axis_index("grp")
    tp = lax.axis_index("tp")
    core = tp % 2
    chip = tp // 2
    chips = tp_count // 2
    y_hi = me // ring
    z = me % ring
    y = y_hi * 2 + pool
    far = ring // 2
    tokens = sk_ref.shape[0]
    prompt = pk_ref.shape[0]
    chunk = prompt // 2
    half_heads = HEADS_DEV // 2
    half_width = half_heads * HD
    half = tokens * half_heads
    right = y_hi * ring + (z + 1) % ring
    left = y_hi * ring + (z + ring - 1) % ring
    up_y = (y + 1) % 4
    down_y = (y + 3) % 4
    up = {"ctx": (up_y // 2) * ring + z, "grp": up_y % 2}
    down = {"ctx": (down_y // 2) * ring + z, "grp": down_y % 2}

    def remote(src, dst, send, recv, device):
        return pltpu.make_async_remote_copy(
            src_ref=src, dst_ref=dst, send_sem=send, recv_sem=recv, device_id=device, device_id_type=MESH
        )

    def pair(n):
        first = 4 * ((n + 1) // 2) + 2 * ((n + 1) % 2) * ((n + ring - 2) // (ring - 1))
        return first, first + 1 + 2 * (n // (ring - 1))

    def toward(n):
        return {"ctx": left + (right - left) * (n % 2)}

    def back(n):
        return {"ctx": right + (left - right) * (n % 2)}

    def whole_copy(n, src):
        u = pair(n)[0]
        return remote(src, qbuf.at[pl.ds(u, 2)], q_send.at[n], q_recv.at[n], toward(n))

    def half_copy(u, src):
        k = ring - 1 + (u % 4) // 3
        return remote(src, qbuf.at[u], q_send.at[k], q_recv.at[k], {"ctx": right + (left - right) * ((u % 4) // 3)})

    def span_copy(k):
        return remote(skv, gath.at[z, y_hi], s_send.at[k], s_recv.at[k], (up, down)[k])

    def span_relay():
        return remote(gath.at[z, down_y // 2], skv_par, sp_send.at[0], sp_recv.at[0], up)

    def gather_copy(i, at):
        return remote(gath.at[at], gath.at[at], g_send.at[i], g_recv.at[i], toward(i))

    def gather_z(i):
        return (z - (2 * (i % 2) - 1) * ((i + 1) // 2) + ring) % ring

    def piece_copy(p):
        src = (pk_ref if p // 2 == 0 else pv_ref).at[pl.ds((p % 2) * chunk, chunk)]
        return remote(src, rel.at[p], r_send.at[p], r_recv.at[p], (up, down)[p % 2])

    def piece_relay(p):
        return remote(rel.at[p], par.at[p], f_send.at[p], f_recv.at[p], (up, down)[p % 2])

    def forward_piece(p):
        piece_copy(p).wait_recv()
        piece_relay(p).start()

    loads = [
        pltpu.make_async_copy(pk_ref, k_raw, load.at[0]),
        pltpu.make_async_copy(pv_ref, v_own.at[:, pl.ds(0, HD)], load.at[1]),
        pltpu.make_async_copy(q_ref.at[:, pl.ds(0, half_width)], qbuf.at[0], load.at[2]),
        pltpu.make_async_copy(q_ref.at[:, pl.ds(half_width, half_width)], qbuf.at[1], load.at[3]),
        pltpu.make_async_copy(ck_hbm, ck, load.at[4]),
        pltpu.make_async_copy(cv_hbm, cv, load.at[5]),
        pltpu.make_async_copy(w_hbm, w, load.at[6]),
    ]
    for item in loads[:4]:
        item.start()

    other_core = {"tp": tp + 1 - 2 * core}
    other_chips = [{"tp": 2 * ((chip + k) % chips) + core} for k in range(1, chips)]
    barrier = pltpu.get_barrier_semaphore()
    for device in [{"ctx": right}, {"ctx": left}, up, down, other_core] + other_chips:
        pl.semaphore_signal(barrier, inc=1, device_id=device, device_id_type=MESH)
    skv[0:tokens, :] = sk_ref[...]
    skv[tokens : 2 * tokens, :] = sv_ref[...]
    for item in loads[2:4]:
        item.wait()
    pl.semaphore_wait(barrier, 4 + chips)

    whole_copy(1, qbuf.at[pl.ds(0, 2)]).start()
    whole_copy(2, qbuf.at[pl.ds(0, 2)]).start()
    for p in range(PIECES):
        piece_copy(p).start()
    span_copy(0).start()
    span_copy(1).start()
    for item in loads[4:]:
        item.start()

    v_own[:, HD : 2 * HD] = jnp.ones((prompt, HD), BF)
    v_par[:, HD : 2 * HD] = jnp.ones((v_par.shape[0], HD), BF)
    for item in loads[:2]:
        item.wait()

    def put_keys(dst, at, rows):
        turned = rows.T
        size = rows.shape[0]
        dst[0:HD, at : at + size] = turned
        dst[HD : 2 * HD, at : at + size] = turned

    for c in range(4):
        put_keys(k_own, c * (prompt // 4), k_raw[c * (prompt // 4) : (c + 1) * (prompt // 4)])

    def queries_of(u):
        parts = [qbuf[u, :, h * HD : (h + 1) * HD] for h in range(half_heads)]
        return split_query(jnp.concatenate(parts, axis=0))

    def attend(halves, keys, values, span):
        total = keys.shape[1]
        tiles = [(a, min(TILE, total - a)) for a in range(0, total, TILE)]
        queries = [queries_of(u) for u in halves]
        top = [None, None]
        before = [None, None]
        out = [None, None]

        def score(b, a, size):
            s = dot_nn(queries[b], keys[:, a : a + size])
            if span and a == prompt:
                r = halves[b] % 4
                query_z = (z - (1 - 2 * (r // 2)) * (halves[b] // 4) + 2 * ring) % ring
                query_ctx = y_hi * ring + query_z
                partner = (1 - y_hi) * ring + z
                token = low_bits(lax.broadcasted_iota(jnp.int32, (half, 2 * tokens), 0), tokens)
                key = lax.broadcasted_iota(jnp.int32, (half, 2 * tokens), 1)
                key_pos = jnp.where(key < tokens, me * tokens + key, partner * tokens + key - tokens)
                s = jnp.where(key_pos <= query_ctx * tokens + token, s, NEG)
            scores[b, :, a : a + size] = s
            for c in range(0, size, HD):
                part_of = s[:, c : c + HD]
                top[b] = part_of if top[b] is None else jnp.maximum(top[b], part_of)

        def settle(b):
            top[b] = jnp.max(top[b], axis=1, keepdims=True)
            if span:
                before[b] = mx[halves[b], :, 0:1]
                top[b] = jnp.maximum(top[b], before[b])

        def weigh(b, a, size):
            weights[b, :, a : a + size] = jnp.exp2(scores[b, :, a : a + size] - top[b]).astype(BF)

        def blend(b, a, size):
            piece = dot_nn(weights[b, :, a : a + size], values[a : a + size, :])
            out[b] = piece if out[b] is None else out[b] + piece

        wide = [(a, min(2 * TILE, total - a)) for a in range(0, total, 2 * TILE)]
        for tile in tiles:
            score(0, *tile)
        settle(0)
        for tile in tiles:
            score(1, *tile)
            weigh(0, *tile)
        settle(1)
        for j, tile in enumerate(tiles):
            if j % 2 == 0:
                blend(0, *wide[j // 2])
            weigh(1, *tile)
        for tile in wide:
            blend(1, *tile)
        for b, u in enumerate(halves):
            if span:
                keep = jnp.exp2(before[b] - top[b])
                acc[u] = acc[u] * keep + out[b][:, 0:HD]
                sm[u] = sm[u] * keep + out[b][:, HD : 2 * HD]
            else:
                acc[u] = out[b][:, 0:HD]
                sm[u] = out[b][:, HD : 2 * HD]
            mx[u] = jnp.broadcast_to(top[b], (half, HD))

    def own_step(n, carry):
        halves = pair(n)

        @pl.when(jnp.logical_and(n > 0, n < ring - 1))
        def _():
            whole_copy(n, qbuf.at[pl.ds(0, 2)]).wait_recv()

        @pl.when(n == ring - 1)
        def _():
            for u in (4 * far, 4 * far + 3):
                half_copy(u, qbuf.at[0]).wait_recv()

        @pl.when(jnp.logical_and(n > 0, n + 2 < ring - 1))
        def _():
            whole_copy(n + 2, qbuf.at[pl.ds(halves[0], 2)]).start()

        @pl.when(n == ring - 3)
        def _():
            half_copy(4 * far, qbuf.at[4 * far - 4]).start()

        @pl.when(n == ring - 2)
        def _():
            half_copy(4 * far + 3, qbuf.at[4 * far - 1]).start()

        attend(halves, k_own, v_own, False)

        @pl.when(n == 0)
        def _():
            for k in range(2):
                span_copy(k).wait_recv()
            span_relay().start()
            gather_copy(1, z).start()
            gather_copy(2, z).start()

        for p in range(2):
            @pl.when(n == ring // 2 + p)
            def _():
                forward_piece(p)

        @pl.when(n > 0)
        def _():
            at = gather_z(n)
            gather_copy(n, at).wait_recv()

            @pl.when(n + 2 < ring)
            def _():
                gather_copy(n + 2, at).start()

        return carry

    lax.fori_loop(0, ring, own_step, 0)
    for p in range(2, PIECES):
        forward_piece(p)

    each = tokens // tp_count
    parts = part.shape[1]
    wide_part = part.shape[5]
    step = min(512, wide_part)
    width = w.shape[1] // 2

    def core_copy(which, j):
        return remote(part.at[which, j, 1 - core], sib.at[which, j], c_send.at[which, j], c_recv.at[which, j], other_core)

    def chip_copy(which, j, k):
        return remote(
            pairs.at[which, j, (chip + k) % chips],
            got.at[which, j, k],
            p_send.at[which, j, k],
            p_recv.at[which, j, k],
            other_chips[k - 1],
        )

    def project(which):
        for j in range(parts):
            def columns(i, carry):
                at = pl.multiple_of(i * step, step)
                from_w = pl.multiple_of(at + j * wide_part, step)
                first = dot_nn(att[...], w[:, pl.ds(from_w, step)])
                second = dot_nn(att[...], w[:, pl.ds(pl.multiple_of(from_w + width, step), step)])
                for k in range(tp_count):
                    rows_of = slice(k * each, (k + 1) * each)
                    both = jnp.concatenate([first[rows_of], second[rows_of]], axis=0).astype(BF)
                    part[which, j, k % 2, k // 2, :, pl.ds(at, step)] = both
                return carry

            lax.fori_loop(0, wide_part // step, columns, 0)
            core_copy(which, j).start()

    def add_cores(which, j):
        core_copy(which, j).wait_recv()
        pairs[which, j] = (part[which, j, core].astype(F32) + sib[which, j].astype(F32)).astype(BF)
        for k in range(1, chips):
            chip_copy(which, j, k).start()

    def summed(which, j):
        total = part[which, j, core, chip].astype(F32) + sib[which, j, chip].astype(F32)
        for k in range(1, chips):
            chip_copy(which, j, k).wait_recv()
            total = total + got[which, j, k].astype(F32)
        return total

    for item in loads[4:]:
        item.wait()

    ctx_count = 2 * ring
    span_total = ctx_count * tokens
    blocks = owner_ref.shape[1]
    per_dev = tokens // BLOCK
    token_at = lax.broadcasted_iota(jnp.int32, (blocks, span_total), 1)
    block_at = lax.broadcasted_iota(jnp.int32, (blocks, span_total), 0)
    ring_at = high_bits(token_at, 2 * tokens)
    side_at = low_bits(high_bits(token_at, tokens), 2)
    block_of = (side_at * ring + ring_at) * per_dev + high_bits(low_bits(token_at, tokens), BLOCK)
    expand = jnp.where(block_of == block_at, 1.0, 0.0).astype(BF)
    other = 1 - pool
    owner_row = jnp.where(other == 0, owner_ref[0:1, :], owner_ref[1:2, :])
    slot_row = jnp.where(other == 0, slot_ref[0:1, :], slot_ref[1:2, :])
    owners = dot_nn(jnp.broadcast_to(owner_row, (8, blocks)).astype(F32).astype(BF), expand)[0:1, :]
    slots = dot_nn(jnp.broadcast_to(slot_row, (8, blocks)).astype(F32).astype(BF), expand)[0:1, :]
    slot_tokens = SLOTS * BLOCK
    wanted = jnp.where(owners == me.astype(F32), slots, -1.0).astype(jnp.int32)
    source = lax.broadcasted_iota(jnp.int32, (1, span_total), 1)
    wanted = wanted * BLOCK + low_bits(source, BLOCK)
    place = lax.broadcasted_iota(jnp.int32, (slot_tokens, span_total), 0)
    picked = jnp.where(place == wanted, 1.0, 0.0).astype(BF)
    gath_k = gath[:, :, 0:tokens, :].reshape(span_total, HD)
    gath_v = gath[:, :, tokens : 2 * tokens, :].reshape(span_total, HD)
    slot_k = dot_nn(picked, gath_k).astype(BF)
    slot_v = dot_nn(picked, gath_v).astype(BF)
    filled = dot_nt(jnp.ones((8, span_total), BF), picked)[0:1, :]

    steps = 4
    group = BLOCK // steps
    cache = ck.shape[1]
    new_pad = jnp.zeros((HD - dk_ref.shape[0], HD), BF)
    dec_rows = HEADS_DEV * BLOCK
    row_id = low_bits(lax.broadcasted_iota(jnp.int32, (dec_rows, HD), 0), BLOCK)
    col_id = lax.broadcasted_iota(jnp.int32, (dec_rows, HD), 1)
    crow_id = high_bits(low_bits(lax.broadcasted_iota(jnp.int32, (dec_rows, group * cache), 0), BLOCK), steps)
    ccol_id = high_bits(lax.broadcasted_iota(jnp.int32, (dec_rows, group * cache), 1), cache)
    one_row = lax.broadcasted_iota(jnp.int32, (1, group * cache), 1)

    def decode_group(g, carry):
        at = pl.ds(pl.multiple_of(g * BLOCK, BLOCK), BLOCK)
        asked = dq_ref[pl.ds(g * group, group)].astype(F32).reshape(BLOCK, HEADS_DEV * HD)
        queries = jnp.concatenate([asked[:, h * HD : (h + 1) * HD] for h in range(HEADS_DEV)], axis=0).astype(BF)
        keys = jnp.concatenate(
            [ck[pl.ds(g * group, group)].reshape(group * cache, HD), slot_k, dk_ref[...], new_pad], axis=0
        )
        values = jnp.concatenate(
            [cv[pl.ds(g * group, group)].reshape(group * cache, HD), slot_v, dv_ref[...], new_pad], axis=0
        )
        raw = dot_nt(queries, keys) * SCALE2
        live = jnp.zeros((1, group * cache), jnp.int32)
        for r in range(group):
            live = jnp.where(high_bits(one_row, cache) == r, len_ref[0, g * group + r], live)
        key_row = jnp.where(low_bits(one_row, cache) < live, high_bits(one_row, cache), -1)
        s_cache = jnp.where(crow_id == key_row, raw[:, 0 : group * cache], NEG)
        s_slot = jnp.where(filled > 0.5, raw[:, group * cache : group * cache + slot_tokens], NEG)
        here = g * BLOCK + row_id
        see_new = (high_bits(here, steps) == high_bits(col_id, steps)) & (col_id <= here)
        s_new = jnp.where(see_new, raw[:, group * cache + slot_tokens :], NEG)
        masked = jnp.concatenate([s_cache, s_slot, s_new], axis=1)
        top = jnp.max(masked, axis=1, keepdims=True)
        shares = jnp.exp2(masked - top)
        total = jnp.sum(shares, axis=1, keepdims=True)
        out = (dot_nn(shares.astype(BF), values) / total).astype(BF)
        for h in range(HEADS_DEV):
            att[at, h * HD : (h + 1) * HD] = out[h * BLOCK : (h + 1) * BLOCK]
        return carry

    lax.fori_loop(0, dq_ref.shape[0] // group, decode_group, 0)
    project(1)

    span_relay().wait_recv()
    span = 2 * tokens
    put_keys(k_par, prompt, jnp.concatenate([sk_ref[...], skv_par[0:tokens, :]], axis=0))
    v_par[prompt : prompt + tokens, 0:HD] = sv_ref[...]
    v_par[prompt + tokens : prompt + span, 0:HD] = skv_par[tokens:span, :]
    for j in range(parts):
        add_cores(1, j)
    for p in range(PIECES):
        piece_relay(p).wait_recv()
        at = (p % 2) * chunk
        if p // 2 == 0:
            for c in range(2):
                put_keys(k_par, at + c * (chunk // 2), par[p, c * (chunk // 2) : (c + 1) * (chunk // 2)])
        else:
            v_par[at : at + chunk, 0:HD] = par[p]

    def out_copy(u):
        return remote(
            obuf.at[u], oin.at[u], o_send.at[u], o_recv.at[u], {"ctx": left + (right - left) * ((u % 4) // 2)}
        )

    lane = lax.broadcasted_iota(jnp.int32, (8, HD), 1)

    def merge(u, box):
        out_copy(box).wait_recv()
        carried = oin[box, half : half + 32, :].astype(F32)
        stats = carried[0:8] + carried[8:16] + carried[16:24]
        for a in range(half // 8):
            in_m[8 * a : 8 * a + 8, :] = jnp.broadcast_to(stats[:, a : a + 1], (8, HD))
            in_l[8 * a : 8 * a + 8, :] = jnp.broadcast_to(stats[:, a + 64 : a + 65], (8, HD))
        top = jnp.maximum(mx[u], in_m[...])
        keep = jnp.exp2(mx[u] - top)
        add = jnp.exp2(in_m[...] - top)
        acc[u] = acc[u] * keep + oin[box, 0:half, :].astype(F32) * add
        sm[u] = sm[u] * keep + in_l[...] * add
        mx[u] = top

    def pack(u):
        obuf[u, 0:half, :] = acc[u].astype(BF)
        stats = jnp.zeros((8, HD), F32)
        for a in range(half // 8):
            at = pl.ds(8 * a, 8)
            stats = jnp.where(lane == a, mx[u, at, :], stats)
            stats = jnp.where(lane == a + 64, sm[u, at, :], stats)
        first = stats.astype(BF).astype(F32)
        second = (stats - first).astype(BF).astype(F32)
        third = stats - first - second
        obuf[u, half : half + 32, :] = jnp.concatenate(
            [first, second, third, jnp.zeros((8, HD), F32)], axis=0
        ).astype(BF)

    def last_step(m, carry):
        n = ring - 1 - m
        halves = pair(n)
        attend(halves, k_par, v_par, True)
        for u in halves:
            d, r = u // 4, u % 4

            @pl.when(jnp.logical_or(d + 1 < far, jnp.logical_and(d + 1 == far, r * (r - 3) == 0)))
            def _():
                merge(u, u + 4)

            pack(u)
            out_copy(u).start()
        return carry

    lax.fori_loop(0, ring - 1, last_step, 0)
    attend((0, 1), k_par, v_par, True)
    for u in range(2):
        merge(u, u + 4)
        merge(u, u + 6)
        done = (acc[u] / sm[u]).astype(BF)
        for h in range(half_heads):
            column = (u * half_heads + h) * HD
            att[:, column : column + HD] = done[h * tokens : (h + 1) * tokens]
    project(0)
    for j in range(parts):
        add_cores(0, j)
    for j in range(parts):
        decode_sum = summed(1, j)
        prefill_sum = summed(0, j)
        for c in range(2):
            rows_of = slice(c * each, (c + 1) * each)
            both = jnp.concatenate([prefill_sum[rows_of], decode_sum[rows_of]], axis=0).astype(BF)
            out_ref[:, c * width + j * wide_part : c * width + (j + 1) * wide_part] = both

    for n in range(1, ring - 1):
        whole_copy(n, qbuf.at[pl.ds(0, 2)]).wait_send()
        for u in pair(n):
            out_copy(u).wait_send()
    for u in (4 * far, 4 * far + 3):
        half_copy(u, qbuf.at[0]).wait_send()
        out_copy(u).wait_send()
    for k in range(2):
        span_copy(k).wait_send()
    span_relay().wait_send()
    for i in range(1, ring):
        gather_copy(i, z).wait_send()
    for p in range(PIECES):
        piece_copy(p).wait_send()
        piece_relay(p).wait_send()
    for which in range(2):
        for j in range(parts):
            core_copy(which, j).wait_send()
            for k in range(1, chips):
                chip_copy(which, j, k).wait_send()


def separate(sums_ref, prefill_ref, decode_ref):
    each = prefill_ref.shape[0]
    sums = sums_ref[...].astype(F32)
    prefill_ref[...] = sums[0:each].astype(BF)
    steps = decode_ref.shape[1]
    for r in range(decode_ref.shape[0]):
        decode_ref[r] = sums[each + r * steps : each + (r + 1) * steps].astype(BF)


def on_device(
    span_queries,
    span_keys,
    span_values,
    prompt_keys,
    prompt_values,
    block_owner,
    block_slot,
    decode_queries,
    decode_new_keys,
    decode_new_values,
    cache_keys,
    cache_values,
    cache_len,
    out_weight,
):
    ring = lax.axis_size("ctx") // 2
    tp_count = lax.axis_size("tp")
    tokens = span_queries.shape[1]
    width = span_queries.shape[2]
    prompt = prompt_keys.shape[1]
    row_count, step_count = decode_queries.shape[1:3]
    cache = cache_keys.shape[2]
    columns = out_weight.shape[1]
    each = tokens // tp_count
    count = 4 * (ring // 2) + 4
    half = tokens * HEADS_DEV // 2
    parts = 2
    wide_part = columns // 2 // parts
    chips = tp_count // 2
    span = 2 * tokens
    total = prompt + span
    vmem = pl.BlockSpec(memory_space=pltpu.VMEM)
    smem = pl.BlockSpec(memory_space=pltpu.SMEM)
    anywhere = pl.BlockSpec(memory_space=pl.ANY)
    dma = pltpu.SemaphoreType.DMA
    sums = pl.pallas_call(
        lambda *refs: kernel(ring, tp_count, *refs),
        out_shape=jax.ShapeDtypeStruct((2 * each, columns), BF),
        in_specs=[anywhere, vmem, vmem, anywhere, anywhere] + [vmem] * 5 + [anywhere, anywhere, smem, anywhere],
        out_specs=vmem,
        scratch_shapes=[
            pltpu.VMEM((count, tokens, width // 2), BF),
            pltpu.VMEM((span, HD), BF),
            pltpu.VMEM((span, HD), BF),
            pltpu.VMEM((ring, 2, span, HD), BF),
            pltpu.VMEM((PIECES, prompt // 2, HD), BF),
            pltpu.VMEM((PIECES, prompt // 2, HD), BF),
            pltpu.VMEM((prompt, HD), BF),
            pltpu.VMEM((2 * HD, prompt), BF),
            pltpu.VMEM((prompt, 2 * HD), BF),
            pltpu.VMEM((2 * HD, total), BF),
            pltpu.VMEM((total, 2 * HD), BF),
            pltpu.VMEM((2, half, total), F32),
            pltpu.VMEM((2, half, total), BF),
            pltpu.VMEM((count, half, HD), F32),
            pltpu.VMEM((count, half, HD), F32),
            pltpu.VMEM((count, half, HD), F32),
            pltpu.VMEM((half, HD), F32),
            pltpu.VMEM((half, HD), F32),
            pltpu.VMEM((count, half + 32, HD), BF),
            pltpu.VMEM((count, half + 32, HD), BF),
            pltpu.VMEM((width, columns), BF),
            pltpu.VMEM((row_count, cache, HD), BF),
            pltpu.VMEM((row_count, cache, HD), BF),
            pltpu.VMEM((tokens, width), BF),
            pltpu.VMEM((2, parts, 2, chips, 2 * each, wide_part), BF),
            pltpu.VMEM((2, parts, chips, 2 * each, wide_part), BF),
            pltpu.VMEM((2, parts, chips, 2 * each, wide_part), BF),
            pltpu.VMEM((2, parts, chips, 2 * each, wide_part), BF),
            dma((ring + 1,)),
            dma((ring + 1,)),
            dma((2,)),
            dma((2,)),
            dma((1,)),
            dma((1,)),
            dma((ring,)),
            dma((ring,)),
            dma((PIECES,)),
            dma((PIECES,)),
            dma((PIECES,)),
            dma((PIECES,)),
            dma((count,)),
            dma((count,)),
            dma((2, parts)),
            dma((2, parts)),
            dma((2, parts, chips)),
            dma((2, parts, chips)),
            dma((7,)),
        ],
        compiler_params=pltpu.CompilerParams(
            collective_id=0, has_side_effects=True, vmem_limit_bytes=60 * 1024 * 1024
        ),
        name="serve",
    )(
        span_queries[0],
        span_keys[0],
        span_values[0],
        prompt_keys[0],
        prompt_values[0],
        block_owner,
        block_slot,
        decode_queries[0],
        decode_new_keys.reshape(row_count * step_count, HD),
        decode_new_values.reshape(row_count * step_count, HD),
        cache_keys[0],
        cache_values[0],
        cache_len,
        out_weight,
    )
    prefill, decode = pl.pallas_call(
        separate,
        out_shape=(
            jax.ShapeDtypeStruct((each, columns), BF),
            jax.ShapeDtypeStruct((row_count // tp_count, step_count, columns), BF),
        ),
        in_specs=[vmem],
        out_specs=(vmem, vmem),
        name="separate",
    )(sums)
    return (prefill[None], decode[None])


def solution(mesh):
    in_specs = (
        P("grp", "ctx", "tp"),
        P("grp", "ctx", "tp"),
        P("grp", "ctx", "tp"),
        P("grp", "ctx", "tp"),
        P("grp", "ctx", "tp"),
        P(),
        P(),
        P("grp", "ctx", None, "tp"),
        P("grp", "ctx", None, "tp"),
        P("grp", "ctx", None, "tp"),
        P("grp", "ctx", None, "tp"),
        P("grp", "ctx", None, "tp"),
        P("grp", "ctx"),
        P("tp", None),
    )
    out_specs = (P("grp", ("ctx", "tp"), None), P("grp", ("ctx", "tp"), None, None))
    return jax.shard_map(
        on_device, mesh=mesh, in_specs=in_specs, out_specs=out_specs, check_vma=False
    )
```

time: 82.8 us -> 84.8 us (1.024)
  Pallas kernels: 82.1 us -> 84 us
    pallas_call x1, Pallas kernels: 80.5 us -> 82.5 us  [on_device(): pl.pallas_call(lambda *refs: kernel(ring, tp_count, *refs), out_shape=jax...]
where the time goes in v3:
time: 84.8 us; the launch traced here: 84.7 us
  Pallas kernels  84 us (99%)
    pallas_call x1, Pallas kernels, on_device(): pl.pallas_call(lambda *refs: kernel(ring, tp_count, *refs), out_shape=jax...  82.5 us

profile of v3, /device:TPU:1, one launch (start us, length us, event | category | flops | bytes accessed | tf_op | source)
XLA Modules:
  0.0 84.7 jit_solution(5672866743993289402)
XLA Ops:
  0.6 82.5 %serve.1.sums_ref = bf16[16,4096]{1,0:T(8,128)(2,1)} custom-call(bf16[64,1024]{1,0:T(8,128)(2,1)} %bitcast.16, bf16[64,128]{1,0:T(8,128)(2,1)} %bitcast.18, bf16[64,128]{1,0:T(8,128)(2,1)} %bitcast.19, bf16[2048,128]{1,0:T(8,128)(2,1)} %bitcast.14, bf16[2048,128]{1,0:T(8,128)(2,1)} %bitcast.15, s32[2,64]{1,0:T(2,128)} %refs_5_.1, s32[2,64]{1,0:T(2,128)} %refs_6_.1, ...), custom_call_target="tpu_custom_call" | custom-call | tf_op jit(solution)/shard_map/serve/pallas_call | solution.py:563
  83.1 1.6 %separate.1 = (bf16[8,4096]{1,0:T(8,128)(2,1)}, bf16[2,4,4096]{2,1,0:T(4,128)(2,1)}) custom-call(bf16[16,4096]{1,0:T(8,128)(2,1)} %serve.1.sums_ref), custom_call_target="tpu_custom_call" | custom-call | tf_op jit(solution)/shard_map/separate/pallas_call | solution.py:637

commit v4 on v3

--- a/solution.py
+++ b/solution.py
@@ -11,8 +11,7 @@
 BLOCK = 16
 SLOTS = 8
 HEADS_DEV = 8
-PIECES = 4
-TILE = 256
+PIECES = 8
 NEG = -1e30
 SCALE2 = HD**-0.5 * math.log2(math.e)
 MESH = pl.DeviceIdType.MESH
@@ -47,7 +46,7 @@
     ring, tp_count,
     q_ref, sk_ref, sv_ref, pk_ref, pv_ref, owner_ref, slot_ref, dq_ref, dk_ref, dv_ref, ck_hbm, cv_hbm, len_ref, w_hbm,
     out_ref,
-    qbuf, skv, skv_par, gath, rel, par, k_raw, k_own, v_own, k_par, v_par, scores, weights,
+    qbuf, skv, skv_par, gath, rel, par, k_raw, v_raw, k_own, v_own, k_par, v_par,
     acc, mx, sm, in_m, in_l, obuf, oin,
     w, ck, cv, att, part, sib, pairs, got,
     q_send, q_recv, s_send, s_recv, sp_send, sp_recv, g_send, g_recv, r_send, r_recv, f_send, f_recv,
@@ -65,7 +64,7 @@
     far = ring // 2
     tokens = sk_ref.shape[0]
     prompt = pk_ref.shape[0]
-    chunk = prompt // 2
+    chunk = prompt // 4
     half_heads = HEADS_DEV // 2
     half_width = half_heads * HD
     half = tokens * half_heads
@@ -111,8 +110,11 @@
     def gather_z(i):
         return (z - (2 * (i % 2) - 1) * ((i + 1) // 2) + ring) % ring
 
+    def piece_rows(p):
+        return ((p % 2) * 2 + p // 4) * chunk
+
     def piece_copy(p):
-        src = (pk_ref if p // 2 == 0 else pv_ref).at[pl.ds((p % 2) * chunk, chunk)]
+        src = (k_raw if (p // 2) % 2 == 0 else v_raw).at[pl.ds(piece_rows(p), chunk)]
         return remote(src, rel.at[p], r_send.at[p], r_recv.at[p], (up, down)[p % 2])
 
     def piece_relay(p):
@@ -124,7 +126,7 @@
 
     loads = [
         pltpu.make_async_copy(pk_ref, k_raw, load.at[0]),
-        pltpu.make_async_copy(pv_ref, v_own.at[:, pl.ds(0, HD)], load.at[1]),
+        pltpu.make_async_copy(pv_ref, v_raw, load.at[1]),
         pltpu.make_async_copy(q_ref.at[:, pl.ds(0, half_width)], qbuf.at[0], load.at[2]),
         pltpu.make_async_copy(q_ref.at[:, pl.ds(half_width, half_width)], qbuf.at[1], load.at[3]),
         pltpu.make_async_copy(ck_hbm, ck, load.at[4]),
@@ -141,7 +143,7 @@
         pl.semaphore_signal(barrier, inc=1, device_id=device, device_id_type=MESH)
     skv[0:tokens, :] = sk_ref[...]
     skv[tokens : 2 * tokens, :] = sv_ref[...]
-    for item in loads[2:4]:
+    for item in loads[:4]:
         item.wait()
     pl.semaphore_wait(barrier, 4 + chips)
 
@@ -154,110 +156,77 @@
     for item in loads[4:]:
         item.start()
 
+    def put_keys(dst, at, rows):
+        size = rows.shape[0]
+        dst[at : at + size, 0:HD] = rows
+        dst[at : at + size, HD : 2 * HD] = rows
+
+    put_keys(k_own, 0, k_raw[...])
+    v_own[:, 0:HD] = v_raw[...]
     v_own[:, HD : 2 * HD] = jnp.ones((prompt, HD), BF)
     v_par[:, HD : 2 * HD] = jnp.ones((v_par.shape[0], HD), BF)
-    for item in loads[:2]:
-        item.wait()
-
-    def put_keys(dst, at, rows):
-        turned = rows.T
-        size = rows.shape[0]
-        dst[0:HD, at : at + size] = turned
-        dst[HD : 2 * HD, at : at + size] = turned
-
-    for c in range(4):
-        put_keys(k_own, c * (prompt // 4), k_raw[c * (prompt // 4) : (c + 1) * (prompt // 4)])
 
     def queries_of(u):
         parts = [qbuf[u, :, h * HD : (h + 1) * HD] for h in range(half_heads)]
         return split_query(jnp.concatenate(parts, axis=0))
 
-    def attend(halves, keys, values, span):
-        total = keys.shape[1]
-        tiles = [(a, min(TILE, total - a)) for a in range(0, total, TILE)]
-        queries = [queries_of(u) for u in halves]
-        top = [None, None]
-        before = [None, None]
-        out = [None, None]
-
-        def score(b, a, size):
-            s = dot_nn(queries[b], keys[:, a : a + size])
-            if span and a == prompt:
-                r = halves[b] % 4
-                query_z = (z - (1 - 2 * (r // 2)) * (halves[b] // 4) + 2 * ring) % ring
-                query_ctx = y_hi * ring + query_z
-                partner = (1 - y_hi) * ring + z
-                token = low_bits(lax.broadcasted_iota(jnp.int32, (half, 2 * tokens), 0), tokens)
-                key = lax.broadcasted_iota(jnp.int32, (half, 2 * tokens), 1)
-                key_pos = jnp.where(key < tokens, me * tokens + key, partner * tokens + key - tokens)
-                s = jnp.where(key_pos <= query_ctx * tokens + token, s, NEG)
-            scores[b, :, a : a + size] = s
-            for c in range(0, size, HD):
-                part_of = s[:, c : c + HD]
-                top[b] = part_of if top[b] is None else jnp.maximum(top[b], part_of)
-
-        def settle(b):
-            top[b] = jnp.max(top[b], axis=1, keepdims=True)
-            if span:
-                before[b] = mx[halves[b], :, 0:1]
-                top[b] = jnp.maximum(top[b], before[b])
-
-        def weigh(b, a, size):
-            weights[b, :, a : a + size] = jnp.exp2(scores[b, :, a : a + size] - top[b]).astype(BF)
-
-        def blend(b, a, size):
-            piece = dot_nn(weights[b, :, a : a + size], values[a : a + size, :])
-            out[b] = piece if out[b] is None else out[b] + piece
-
-        wide = [(a, min(2 * TILE, total - a)) for a in range(0, total, 2 * TILE)]
-        for tile in tiles:
-            score(0, *tile)
-        settle(0)
-        for tile in tiles:
-            score(1, *tile)
-            weigh(0, *tile)
-        settle(1)
-        for j, tile in enumerate(tiles):
-            if j % 2 == 0:
-                blend(0, *wide[j // 2])
-            weigh(1, *tile)
-        for tile in wide:
-            blend(1, *tile)
-        for b, u in enumerate(halves):
-            if span:
-                keep = jnp.exp2(before[b] - top[b])
-                acc[u] = acc[u] * keep + out[b][:, 0:HD]
-                sm[u] = sm[u] * keep + out[b][:, HD : 2 * HD]
-            else:
-                acc[u] = out[b][:, 0:HD]
-                sm[u] = out[b][:, HD : 2 * HD]
-            mx[u] = jnp.broadcast_to(top[b], (half, HD))
+    def attend_own(halves):
+        for u in halves:
+            scores = dot_nt(queries_of(u), k_own[...])
+            top = jnp.max(scores, axis=1, keepdims=True)
+            out = dot_nn(jnp.exp2(scores - top).astype(BF), v_own[...])
+            mx[u] = jnp.broadcast_to(top, (half, HD))
+            acc[u] = out[:, 0:HD]
+            sm[u] = out[:, HD : 2 * HD]
+
+    def attend_partner(halves):
+        for u in halves:
+            query_z = (z - (1 - 2 * ((u % 4) // 2)) * (u // 4) + 2 * ring) % ring
+            query_ctx = y_hi * ring + query_z
+            partner = (1 - y_hi) * ring + z
+            scores = dot_nt(queries_of(u), k_par[...])
+            token = low_bits(lax.broadcasted_iota(jnp.int32, (half, 2 * tokens), 0), tokens)
+            key = lax.broadcasted_iota(jnp.int32, (half, 2 * tokens), 1)
+            key_pos = jnp.where(key < tokens, me * tokens + key, partner * tokens + key - tokens)
+            seen = jnp.where(key_pos <= query_ctx * tokens + token, scores[:, prompt:], NEG)
+            before = mx[u, :, 0:1]
+            top = jnp.maximum(
+                jnp.max(scores[:, 0:prompt], axis=1, keepdims=True), jnp.max(seen, axis=1, keepdims=True)
+            )
+            top = jnp.maximum(top, before)
+            weights = jnp.concatenate(
+                [jnp.exp2(scores[:, 0:prompt] - top).astype(BF), jnp.exp2(seen - top).astype(BF)], axis=1
+            )
+            out = dot_nn(weights, v_par[...])
+            keep = jnp.exp2(before - top)
+            mx[u] = jnp.broadcast_to(top, (half, HD))
+            acc[u] = acc[u] * keep + out[:, 0:HD]
+            sm[u] = sm[u] * keep + out[:, HD : 2 * HD]
 
     def own_step(n, carry):
         halves = pair(n)
 
-        @pl.when(jnp.logical_and(n > 0, n < ring - 1))
+        @pl.when(jnp.logical_and(n % 2 == 1, n < ring - 1))
         def _():
-            whole_copy(n, qbuf.at[pl.ds(0, 2)]).wait_recv()
+            for m in (n, n + 1):
+                whole_copy(m, qbuf.at[pl.ds(0, 2)]).wait_recv()
+
+        @pl.when(jnp.logical_and(n % 2 == 1, n < ring - 3))
+        def _():
+            for m in (n, n + 1):
+                whole_copy(m + 2, qbuf.at[pl.ds(pair(m)[0], 2)]).start()
+
+        @pl.when(n == ring - 3)
+        def _():
+            half_copy(4 * far, qbuf.at[4 * far - 4]).start()
+            half_copy(4 * far + 3, qbuf.at[4 * far - 1]).start()
 
         @pl.when(n == ring - 1)
         def _():
             for u in (4 * far, 4 * far + 3):
                 half_copy(u, qbuf.at[0]).wait_recv()
 
-        @pl.when(jnp.logical_and(n > 0, n + 2 < ring - 1))
-        def _():
-            whole_copy(n + 2, qbuf.at[pl.ds(halves[0], 2)]).start()
-
-        @pl.when(n == ring - 3)
-        def _():
-            half_copy(4 * far, qbuf.at[4 * far - 4]).start()
-
-        @pl.when(n == ring - 2)
-        def _():
-            half_copy(4 * far + 3, qbuf.at[4 * far - 1]).start()
-
-        attend(halves, k_own, v_own, False)
+        attend_own(halves)
 
         @pl.when(n == 0)
         def _():
@@ -267,10 +236,11 @@
             gather_copy(1, z).start()
             gather_copy(2, z).start()
 
-        for p in range(2):
-            @pl.when(n == ring // 2 + p)
+        for c in range(PIECES // 2):
+            @pl.when(n == min(c + 2, ring - 1))
             def _():
-                forward_piece(p)
+                forward_piece(2 * c)
+                forward_piece(2 * c + 1)
 
         @pl.when(n > 0)
         def _():
@@ -284,8 +254,6 @@
         return carry
 
     lax.fori_loop(0, ring, own_step, 0)
-    for p in range(2, PIECES):
-        forward_piece(p)
 
     each = tokens // tp_count
     parts = part.shape[1]
@@ -416,10 +384,9 @@
         add_cores(1, j)
     for p in range(PIECES):
         piece_relay(p).wait_recv()
-        at = (p % 2) * chunk
-        if p // 2 == 0:
-            for c in range(2):
-                put_keys(k_par, at + c * (chunk // 2), par[p, c * (chunk // 2) : (c + 1) * (chunk // 2)])
+        at = piece_rows(p)
+        if (p // 2) % 2 == 0:
+            put_keys(k_par, at, par[p])
         else:
             v_par[at : at + chunk, 0:HD] = par[p]
 
@@ -461,7 +428,7 @@
     def last_step(m, carry):
         n = ring - 1 - m
         halves = pair(n)
-        attend(halves, k_par, v_par, True)
+        attend_partner(halves)
         for u in halves:
             d, r = u // 4, u % 4
 
@@ -474,7 +441,7 @@
         return carry
 
     lax.fori_loop(0, ring - 1, last_step, 0)
-    attend((0, 1), k_par, v_par, True)
+    attend_partner((0, 1))
     for u in range(2):
         merge(u, u + 4)
         merge(u, u + 6)
@@ -570,15 +537,14 @@
             pltpu.VMEM((span, HD), BF),
             pltpu.VMEM((span, HD), BF),
             pltpu.VMEM((ring, 2, span, HD), BF),
-            pltpu.VMEM((PIECES, prompt // 2, HD), BF),
-            pltpu.VMEM((PIECES, prompt // 2, HD), BF),
+            pltpu.VMEM((PIECES, prompt // 4, HD), BF),
+            pltpu.VMEM((PIECES, prompt // 4, HD), BF),
             pltpu.VMEM((prompt, HD), BF),
-            pltpu.VMEM((2 * HD, prompt), BF),
+            pltpu.VMEM((prompt, HD), BF),
             pltpu.VMEM((prompt, 2 * HD), BF),
-            pltpu.VMEM((2 * HD, total), BF),
+            pltpu.VMEM((prompt, 2 * HD), BF),
             pltpu.VMEM((total, 2 * HD), BF),
-            pltpu.VMEM((2, half, total), F32),
-            pltpu.VMEM((2, half, total), BF),
+            pltpu.VMEM((total, 2 * HD), BF),
             pltpu.VMEM((count, half, HD), F32),
             pltpu.VMEM((count, half, HD), F32),
             pltpu.VMEM((count, half, HD), F32),

time: 84.8 us -> 86.7 us (1.022)
  Pallas kernels: 84 us -> 86 us
    pallas_call x1, Pallas kernels: 82.5 us -> 84.4 us  [on_device(): pl.pallas_call(lambda *refs: kernel(ring, tp_count, *refs), out_shape=jax...]
where the time goes in v4:
time: 86.7 us; the launch traced here: 86.6 us
  Pallas kernels  86 us (99%)
    pallas_call x1, Pallas kernels, on_device(): pl.pallas_call(lambda *refs: kernel(ring, tp_count, *refs), out_shape=jax...  84.4 us

profile of v4, /device:TPU:1, one launch (start us, length us, event | category | flops | bytes accessed | tf_op | source)
XLA Modules:
  0.0 86.6 jit_solution(5579742917690388594)
XLA Ops:
  0.6 84.4 %serve.1.sums_ref = bf16[16,4096]{1,0:T(8,128)(2,1)} custom-call(bf16[64,1024]{1,0:T(8,128)(2,1)} %bitcast.16, bf16[64,128]{1,0:T(8,128)(2,1)} %bitcast.18, bf16[64,128]{1,0:T(8,128)(2,1)} %bitcast.19, bf16[2048,128]{1,0:T(8,128)(2,1)} %bitcast.14, bf16[2048,128]{1,0:T(8,128)(2,1)} %bitcast.15, s32[2,64]{1,0:T(2,128)} %refs_5_.1, s32[2,64]{1,0:T(2,128)} %refs_6_.1, ...), custom_call_target="tpu_custom_call" | custom-call | tf_op jit(solution)/shard_map/serve/pallas_call | solution.py:530
  85.0 1.6 %separate.1 = (bf16[8,4096]{1,0:T(8,128)(2,1)}, bf16[2,4,4096]{2,1,0:T(4,128)(2,1)}) custom-call(bf16[16,4096]{1,0:T(8,128)(2,1)} %serve.1.sums_ref), custom_call_target="tpu_custom_call" | custom-call | tf_op jit(solution)/shard_map/separate/pallas_call | solution.py:603

commit v5 on v4

--- a/solution.py
+++ b/solution.py
@@ -61,12 +61,10 @@
     y_hi = me // ring
     z = me % ring
     y = y_hi * 2 + pool
-    far = ring // 2
     tokens = sk_ref.shape[0]
     prompt = pk_ref.shape[0]
     chunk = prompt // 4
     half_heads = HEADS_DEV // 2
-    half_width = half_heads * HD
     half = tokens * half_heads
     right = y_hi * ring + (z + 1) % ring
     left = y_hi * ring + (z + ring - 1) % ring
@@ -80,23 +78,17 @@
             src_ref=src, dst_ref=dst, send_sem=send, recv_sem=recv, device_id=device, device_id_type=MESH
         )
 
-    def pair(n):
-        first = 4 * ((n + 1) // 2) + 2 * ((n + 1) % 2) * ((n + ring - 2) // (ring - 1))
-        return first, first + 1 + 2 * (n // (ring - 1))
-
-    def toward(n):
-        return {"ctx": left + (right - left) * (n % 2)}
-
-    def back(n):
-        return {"ctx": right + (left - right) * (n % 2)}
-
-    def whole_copy(n, src):
-        u = pair(n)[0]
-        return remote(src, qbuf.at[pl.ds(u, 2)], q_send.at[n], q_recv.at[n], toward(n))
-
-    def half_copy(u, src):
-        k = ring - 1 + (u % 4) // 3
-        return remote(src, qbuf.at[u], q_send.at[k], q_recv.at[k], {"ctx": right + (left - right) * ((u % 4) // 3)})
+    def toward(i):
+        return {"ctx": left + (right - left) * (i % 2)}
+
+    def back(i):
+        return {"ctx": right + (left - right) * (i % 2)}
+
+    def source_z(i):
+        return (z - (2 * (i % 2) - 1) * ((i + 1) // 2) + ring) % ring
+
+    def query_copy(i, src):
+        return remote(src, qbuf.at[i], q_send.at[i], q_recv.at[i], toward(i))
 
     def span_copy(k):
         return remote(skv, gath.at[z, y_hi], s_send.at[k], s_recv.at[k], (up, down)[k])
@@ -106,9 +98,6 @@
 
     def gather_copy(i, at):
         return remote(gath.at[at], gath.at[at], g_send.at[i], g_recv.at[i], toward(i))
-
-    def gather_z(i):
-        return (z - (2 * (i % 2) - 1) * ((i + 1) // 2) + ring) % ring
 
     def piece_rows(p):
         return ((p % 2) * 2 + p // 4) * chunk
@@ -127,13 +116,12 @@
     loads = [
         pltpu.make_async_copy(pk_ref, k_raw, load.at[0]),
         pltpu.make_async_copy(pv_ref, v_raw, load.at[1]),
-        pltpu.make_async_copy(q_ref.at[:, pl.ds(0, half_width)], qbuf.at[0], load.at[2]),
-        pltpu.make_async_copy(q_ref.at[:, pl.ds(half_width, half_width)], qbuf.at[1], load.at[3]),
-        pltpu.make_async_copy(ck_hbm, ck, load.at[4]),
-        pltpu.make_async_copy(cv_hbm, cv, load.at[5]),
-        pltpu.make_async_copy(w_hbm, w, load.at[6]),
+        pltpu.make_async_copy(q_ref, qbuf.at[0], load.at[2]),
+        pltpu.make_async_copy(ck_hbm, ck, load.at[3]),
+        pltpu.make_async_copy(cv_hbm, cv, load.at[4]),
+        pltpu.make_async_copy(w_hbm, w, load.at[5]),
     ]
-    for item in loads[:4]:
+    for item in loads[:3]:
         item.start()
 
     other_core = {"tp": tp + 1 - 2 * core}
@@ -143,17 +131,17 @@
         pl.semaphore_signal(barrier, inc=1, device_id=device, device_id_type=MESH)
     skv[0:tokens, :] = sk_ref[...]
     skv[tokens : 2 * tokens, :] = sv_ref[...]
-    for item in loads[:4]:
+    for item in loads[:3]:
         item.wait()
     pl.semaphore_wait(barrier, 4 + chips)
 
-    whole_copy(1, qbuf.at[pl.ds(0, 2)]).start()
-    whole_copy(2, qbuf.at[pl.ds(0, 2)]).start()
+    query_copy(1, qbuf.at[0]).start()
+    query_copy(2, qbuf.at[0]).start()
+    span_copy(0).start()
+    span_copy(1).start()
     for p in range(PIECES):
         piece_copy(p).start()
-    span_copy(0).start()
-    span_copy(1).start()
-    for item in loads[4:]:
+    for item in loads[3:]:
         item.start()
 
     def put_keys(dst, at, rows):
@@ -166,30 +154,38 @@
     v_own[:, HD : 2 * HD] = jnp.ones((prompt, HD), BF)
     v_par[:, HD : 2 * HD] = jnp.ones((v_par.shape[0], HD), BF)
 
-    def queries_of(u):
-        parts = [qbuf[u, :, h * HD : (h + 1) * HD] for h in range(half_heads)]
-        return split_query(jnp.concatenate(parts, axis=0))
-
-    def attend_own(halves):
-        for u in halves:
-            scores = dot_nt(queries_of(u), k_own[...])
+    spans = [pl.ds(0, half), pl.ds(half, half)]
+
+    def queries_of(i):
+        halves = []
+        for b in range(2):
+            heads = range(b * half_heads, (b + 1) * half_heads)
+            halves.append(split_query(jnp.concatenate([qbuf[i, :, h * HD : (h + 1) * HD] for h in heads], axis=0)))
+        return halves
+
+    def attend_own(i):
+        results = []
+        for queries in queries_of(i):
+            scores = dot_nt(queries, k_own[...])
             top = jnp.max(scores, axis=1, keepdims=True)
-            out = dot_nn(jnp.exp2(scores - top).astype(BF), v_own[...])
-            mx[u] = jnp.broadcast_to(top, (half, HD))
-            acc[u] = out[:, 0:HD]
-            sm[u] = out[:, HD : 2 * HD]
-
-    def attend_partner(halves):
-        for u in halves:
-            query_z = (z - (1 - 2 * ((u % 4) // 2)) * (u // 4) + 2 * ring) % ring
-            query_ctx = y_hi * ring + query_z
-            partner = (1 - y_hi) * ring + z
-            scores = dot_nt(queries_of(u), k_par[...])
-            token = low_bits(lax.broadcasted_iota(jnp.int32, (half, 2 * tokens), 0), tokens)
-            key = lax.broadcasted_iota(jnp.int32, (half, 2 * tokens), 1)
-            key_pos = jnp.where(key < tokens, me * tokens + key, partner * tokens + key - tokens)
-            seen = jnp.where(key_pos <= query_ctx * tokens + token, scores[:, prompt:], NEG)
-            before = mx[u, :, 0:1]
+            results.append((top, dot_nn(jnp.exp2(scores - top).astype(BF), v_own[...])))
+        for at, (top, out) in zip(spans, results):
+            mx[i, at, :] = jnp.broadcast_to(top, (half, HD))
+            acc[i, at, :] = out[:, 0:HD]
+            sm[i, at, :] = out[:, HD : 2 * HD]
+
+    def attend_partner(i):
+        query_ctx = y_hi * ring + source_z(i)
+        partner = (1 - y_hi) * ring + z
+        token = low_bits(lax.broadcasted_iota(jnp.int32, (half, 2 * tokens), 0), tokens)
+        key = lax.broadcasted_iota(jnp.int32, (half, 2 * tokens), 1)
+        key_pos = jnp.where(key < tokens, me * tokens + key, partner * tokens + key - tokens)
+        visible = key_pos <= query_ctx * tokens + token
+        befores = [mx[i, at, 0:1] for at in spans]
+        results = []
+        for queries, before in zip(queries_of(i), befores):
+            scores = dot_nt(queries, k_par[...])
+            seen = jnp.where(visible, scores[:, prompt:], NEG)
             top = jnp.maximum(
                 jnp.max(scores[:, 0:prompt], axis=1, keepdims=True), jnp.max(seen, axis=1, keepdims=True)
             )
@@ -197,36 +193,24 @@
             weights = jnp.concatenate(
                 [jnp.exp2(scores[:, 0:prompt] - top).astype(BF), jnp.exp2(seen - top).astype(BF)], axis=1
             )
-            out = dot_nn(weights, v_par[...])
+            results.append((top, dot_nn(weights, v_par[...])))
+        for at, before, (top, out) in zip(spans, befores, results):
             keep = jnp.exp2(before - top)
-            mx[u] = jnp.broadcast_to(top, (half, HD))
-            acc[u] = acc[u] * keep + out[:, 0:HD]
-            sm[u] = sm[u] * keep + out[:, HD : 2 * HD]
+            mx[i, at, :] = jnp.broadcast_to(top, (half, HD))
+            acc[i, at, :] = acc[i, at, :] * keep + out[:, 0:HD]
+            sm[i, at, :] = sm[i, at, :] * keep + out[:, HD : 2 * HD]
 
     def own_step(n, carry):
-        halves = pair(n)
-
-        @pl.when(jnp.logical_and(n % 2 == 1, n < ring - 1))
-        def _():
-            for m in (n, n + 1):
-                whole_copy(m, qbuf.at[pl.ds(0, 2)]).wait_recv()
-
-        @pl.when(jnp.logical_and(n % 2 == 1, n < ring - 3))
-        def _():
-            for m in (n, n + 1):
-                whole_copy(m + 2, qbuf.at[pl.ds(pair(m)[0], 2)]).start()
-
-        @pl.when(n == ring - 3)
-        def _():
-            half_copy(4 * far, qbuf.at[4 * far - 4]).start()
-            half_copy(4 * far + 3, qbuf.at[4 * far - 1]).start()
-
-        @pl.when(n == ring - 1)
-        def _():
-            for u in (4 * far, 4 * far + 3):
-                half_copy(u, qbuf.at[0]).wait_recv()
-
-        attend_own(halves)
+        for c in range(2):
+            @pl.when(jnp.logical_and(n % 2 == 1, n + c < ring))
+            def _():
+                query_copy(n + c, qbuf.at[0]).wait_recv()
+
+            @pl.when(jnp.logical_and(n % 2 == 1, n + c + 2 < ring))
+            def _():
+                query_copy(n + c + 2, qbuf.at[n + c]).start()
+
+        attend_own(n)
 
         @pl.when(n == 0)
         def _():
@@ -244,7 +228,7 @@
 
         @pl.when(n > 0)
         def _():
-            at = gather_z(n)
+            at = source_z(n)
             gather_copy(n, at).wait_recv()
 
             @pl.when(n + 2 < ring)
@@ -302,7 +286,7 @@
             total = total + got[which, j, k].astype(F32)
         return total
 
-    for item in loads[4:]:
+    for item in loads[3:]:
         item.wait()
 
     ctx_count = 2 * ring
@@ -390,65 +374,60 @@
         else:
             v_par[at : at + chunk, 0:HD] = par[p]
 
-    def out_copy(u):
-        return remote(
-            obuf.at[u], oin.at[u], o_send.at[u], o_recv.at[u], {"ctx": left + (right - left) * ((u % 4) // 2)}
-        )
+    rows = 2 * half
+
+    def out_copy(i):
+        return remote(obuf.at[i], oin.at[i], o_send.at[i], o_recv.at[i], back(i))
 
     lane = lax.broadcasted_iota(jnp.int32, (8, HD), 1)
-
-    def merge(u, box):
+    group_lanes = [(8 * a, (a % 8) * 16 + a // 8) for a in range(rows // 8)]
+
+    def merge(i, box):
         out_copy(box).wait_recv()
-        carried = oin[box, half : half + 32, :].astype(F32)
+        carried = oin[box, rows : rows + 32, :].astype(F32)
         stats = carried[0:8] + carried[8:16] + carried[16:24]
-        for a in range(half // 8):
-            in_m[8 * a : 8 * a + 8, :] = jnp.broadcast_to(stats[:, a : a + 1], (8, HD))
-            in_l[8 * a : 8 * a + 8, :] = jnp.broadcast_to(stats[:, a + 64 : a + 65], (8, HD))
-        top = jnp.maximum(mx[u], in_m[...])
-        keep = jnp.exp2(mx[u] - top)
+        for at, a in group_lanes:
+            in_m[at : at + 8, :] = jnp.broadcast_to(stats[:, a : a + 1], (8, HD))
+            in_l[at : at + 8, :] = jnp.broadcast_to(stats[:, a + 8 : a + 9], (8, HD))
+        top = jnp.maximum(mx[i], in_m[...])
+        keep = jnp.exp2(mx[i] - top)
         add = jnp.exp2(in_m[...] - top)
-        acc[u] = acc[u] * keep + oin[box, 0:half, :].astype(F32) * add
-        sm[u] = sm[u] * keep + in_l[...] * add
-        mx[u] = top
-
-    def pack(u):
-        obuf[u, 0:half, :] = acc[u].astype(BF)
+        acc[i] = acc[i] * keep + oin[box, 0:rows, :].astype(F32) * add
+        sm[i] = sm[i] * keep + in_l[...] * add
+        mx[i] = top
+
+    def pack(i):
+        obuf[i, 0:rows, :] = acc[i].astype(BF)
         stats = jnp.zeros((8, HD), F32)
-        for a in range(half // 8):
-            at = pl.ds(8 * a, 8)
-            stats = jnp.where(lane == a, mx[u, at, :], stats)
-            stats = jnp.where(lane == a + 64, sm[u, at, :], stats)
+        for at, a in group_lanes:
+            stats = jnp.where(lane == a, mx[i, pl.ds(at, 8), :], stats)
+            stats = jnp.where(lane == a + 8, sm[i, pl.ds(at, 8), :], stats)
         first = stats.astype(BF).astype(F32)
         second = (stats - first).astype(BF).astype(F32)
         third = stats - first - second
-        obuf[u, half : half + 32, :] = jnp.concatenate(
+        obuf[i, rows : rows + 32, :] = jnp.concatenate(
             [first, second, third, jnp.zeros((8, HD), F32)], axis=0
         ).astype(BF)
 
-    def last_step(m, carry):
-        n = ring - 1 - m
-        halves = pair(n)
-        attend_partner(halves)
-        for u in halves:
-            d, r = u // 4, u % 4
-
-            @pl.when(jnp.logical_or(d + 1 < far, jnp.logical_and(d + 1 == far, r * (r - 3) == 0)))
-            def _():
-                merge(u, u + 4)
-
-            pack(u)
-            out_copy(u).start()
+    def partner_step(m, carry):
+        i = ring - 1 - m
+        attend_partner(i)
+
+        @pl.when(i + 2 < ring)
+        def _():
+            merge(i, i + 2)
+
+        pack(i)
+        out_copy(i).start()
         return carry
 
-    lax.fori_loop(0, ring - 1, last_step, 0)
-    attend_partner((0, 1))
-    for u in range(2):
-        merge(u, u + 4)
-        merge(u, u + 6)
-        done = (acc[u] / sm[u]).astype(BF)
-        for h in range(half_heads):
-            column = (u * half_heads + h) * HD
-            att[:, column : column + HD] = done[h * tokens : (h + 1) * tokens]
+    lax.fori_loop(0, ring - 1, partner_step, 0)
+    attend_partner(0)
+    merge(0, 2)
+    merge(0, 1)
+    done = (acc[0] / sm[0]).astype(BF)
+    for h in range(HEADS_DEV):
+        att[:, h * HD : (h + 1) * HD] = done[h * tokens : (h + 1) * tokens]
     project(0)
     for j in range(parts):
         add_cores(0, j)
@@ -460,13 +439,9 @@
             both = jnp.concatenate([prefill_sum[rows_of], decode_sum[rows_of]], axis=0).astype(BF)
             out_ref[:, c * width + j * wide_part : c * width + (j + 1) * wide_part] = both
 
-    for n in range(1, ring - 1):
-        whole_copy(n, qbuf.at[pl.ds(0, 2)]).wait_send()
-        for u in pair(n):
-            out_copy(u).wait_send()
-    for u in (4 * far, 4 * far + 3):
-        half_copy(u, qbuf.at[0]).wait_send()
-        out_copy(u).wait_send()
+    for i in range(1, ring):
+        query_copy(i, qbuf.at[0]).wait_send()
+        out_copy(i).wait_send()
     for k in range(2):
         span_copy(k).wait_send()
     span_relay().wait_send()
@@ -516,8 +491,7 @@
     cache = cache_keys.shape[2]
     columns = out_weight.shape[1]
     each = tokens // tp_count
-    count = 4 * (ring // 2) + 4
-    half = tokens * HEADS_DEV // 2
+    rows = tokens * HEADS_DEV
     parts = 2
     wide_part = columns // 2 // parts
     chips = tp_count // 2
@@ -533,7 +507,7 @@
         in_specs=[anywhere, vmem, vmem, anywhere, anywhere] + [vmem] * 5 + [anywhere, anywhere, smem, anywhere],
         out_specs=vmem,
         scratch_shapes=[
-            pltpu.VMEM((count, tokens, width // 2), BF),
+            pltpu.VMEM((ring, tokens, width), BF),
             pltpu.VMEM((span, HD), BF),
             pltpu.VMEM((span, HD), BF),
             pltpu.VMEM((ring, 2, span, HD), BF),
@@ -545,13 +519,13 @@
             pltpu.VMEM((prompt, 2 * HD), BF),
             pltpu.VMEM((total, 2 * HD), BF),
             pltpu.VMEM((total, 2 * HD), BF),
-            pltpu.VMEM((count, half, HD), F32),
-            pltpu.VMEM((count, half, HD), F32),
-            pltpu.VMEM((count, half, HD), F32),
-            pltpu.VMEM((half, HD), F32),
-            pltpu.VMEM((half, HD), F32),
-            pltpu.VMEM((count, half + 32, HD), BF),
-            pltpu.VMEM((count, half + 32, HD), BF),
+            pltpu.VMEM((ring, rows, HD), F32),
+            pltpu.VMEM((ring, rows, HD), F32),
+            pltpu.VMEM((ring, rows, HD), F32),
+            pltpu.VMEM((rows, HD), F32),
+            pltpu.VMEM((rows, HD), F32),
+            pltpu.VMEM((ring, rows + 32, HD), BF),
+            pltpu.VMEM((ring, rows + 32, HD), BF),
             pltpu.VMEM((width, columns), BF),
             pltpu.VMEM((row_count, cache, HD), BF),
             pltpu.VMEM((row_count, cache, HD), BF),
@@ -560,8 +534,8 @@
             pltpu.VMEM((2, parts, chips, 2 * each, wide_part), BF),
             pltpu.VMEM((2, parts, chips, 2 * each, wide_part), BF),
             pltpu.VMEM((2, parts, chips, 2 * each, wide_part), BF),
-            dma((ring + 1,)),
-            dma((ring + 1,)),
+            dma((ring,)),
+            dma((ring,)),
             dma((2,)),
             dma((2,)),
             dma((1,)),
@@ -572,13 +546,13 @@
             dma((PIECES,)),
             dma((PIECES,)),
             dma((PIECES,)),
-            dma((count,)),
-            dma((count,)),
+            dma((ring,)),
+            dma((ring,)),
             dma((2, parts)),
             dma((2, parts)),
             dma((2, parts, chips)),
             dma((2, parts, chips)),
-            dma((7,)),
+            dma((6,)),
         ],
         compiler_params=pltpu.CompilerParams(
             collective_id=0, has_side_effects=True, vmem_limit_bytes=60 * 1024 * 1024

time: 86.7 us -> 74.3 us (0.86)
  Pallas kernels: 86 us -> 73.5 us
    pallas_call x1, Pallas kernels: 84.4 us -> 72 us  [on_device(): pl.pallas_call(lambda *refs: kernel(ring, tp_count, *refs), out_shape=jax...]
where the time goes in v5:
time: 74.3 us; the launch traced here: 74.2 us
  Pallas kernels  73.5 us (99%)
    pallas_call x1, Pallas kernels, on_device(): pl.pallas_call(lambda *refs: kernel(ring, tp_count, *refs), out_shape=jax...  72 us
    pallas_call x1, Pallas kernels, on_device(): pl.pallas_call(separate, out_shape=(jax.ShapeDtypeStruct((each, columns),...  1.57 us

profile of v5, /device:TPU:1, one launch (start us, length us, event | category | flops | bytes accessed | tf_op | source)
XLA Modules:
  0.0 74.2 jit_solution(13533716227112703725)
XLA Ops:
  0.6 72.0 %serve.1.sums_ref = bf16[16,4096]{1,0:T(8,128)(2,1)} custom-call(bf16[64,1024]{1,0:T(8,128)(2,1)} %bitcast.16, bf16[64,128]{1,0:T(8,128)(2,1)} %bitcast.18, bf16[64,128]{1,0:T(8,128)(2,1)} %bitcast.19, bf16[2048,128]{1,0:T(8,128)(2,1)} %bitcast.14, bf16[2048,128]{1,0:T(8,128)(2,1)} %bitcast.15, s32[2,64]{1,0:T(2,128)} %refs_5_.1, s32[2,64]{1,0:T(2,128)} %refs_6_.1, ...), custom_call_target="tpu_custom_call" | custom-call | tf_op jit(solution)/shard_map/serve/pallas_call | solution.py:504
  72.6 1.6 %separate.1 = (bf16[8,4096]{1,0:T(8,128)(2,1)}, bf16[2,4,4096]{2,1,0:T(4,128)(2,1)}) custom-call(bf16[16,4096]{1,0:T(8,128)(2,1)} %serve.1.sums_ref), custom_call_target="tpu_custom_call" | custom-call | tf_op jit(solution)/shard_map/separate/pallas_call | solution.py:577

commit v6 on v5

--- a/solution.py
+++ b/solution.py
@@ -27,13 +27,6 @@
     return jnp.dot(a, b, preferred_element_type=F32)
 
 
-def split_query(q):
-    scaled = q.astype(F32) * SCALE2
-    high = scaled.astype(BF)
-    low = (scaled - high.astype(F32)).astype(BF)
-    return jnp.concatenate([high, low], axis=1)
-
-
 def low_bits(x, size):
     return jnp.bitwise_and(x, size - 1)
 
@@ -46,7 +39,7 @@
     ring, tp_count,
     q_ref, sk_ref, sv_ref, pk_ref, pv_ref, owner_ref, slot_ref, dq_ref, dk_ref, dv_ref, ck_hbm, cv_hbm, len_ref, w_hbm,
     out_ref,
-    qbuf, skv, skv_par, gath, rel, par, k_raw, v_raw, k_own, v_own, k_par, v_par,
+    qbuf, skv, skv_par, gath, rel, k_own, v_own, k_par, v_par,
     acc, mx, sm, in_m, in_l, obuf, oin,
     w, ck, cv, att, part, sib, pairs, got,
     q_send, q_recv, s_send, s_recv, sp_send, sp_recv, g_send, g_recv, r_send, r_recv, f_send, f_recv,
@@ -64,8 +57,6 @@
     tokens = sk_ref.shape[0]
     prompt = pk_ref.shape[0]
     chunk = prompt // 4
-    half_heads = HEADS_DEV // 2
-    half = tokens * half_heads
     right = y_hi * ring + (z + 1) % ring
     left = y_hi * ring + (z + ring - 1) % ring
     up_y = (y + 1) % 4
@@ -103,19 +94,20 @@
         return ((p % 2) * 2 + p // 4) * chunk
 
     def piece_copy(p):
-        src = (k_raw if (p // 2) % 2 == 0 else v_raw).at[pl.ds(piece_rows(p), chunk)]
+        src = (k_own if (p // 2) % 2 == 0 else v_own).at[pl.ds(piece_rows(p), chunk)]
         return remote(src, rel.at[p], r_send.at[p], r_recv.at[p], (up, down)[p % 2])
 
     def piece_relay(p):
-        return remote(rel.at[p], par.at[p], f_send.at[p], f_recv.at[p], (up, down)[p % 2])
+        dst = (k_par if (p // 2) % 2 == 0 else v_par).at[pl.ds(piece_rows(p), chunk)]
+        return remote(rel.at[p], dst, f_send.at[p], f_recv.at[p], (up, down)[p % 2])
 
     def forward_piece(p):
         piece_copy(p).wait_recv()
         piece_relay(p).start()
 
     loads = [
-        pltpu.make_async_copy(pk_ref, k_raw, load.at[0]),
-        pltpu.make_async_copy(pv_ref, v_raw, load.at[1]),
+        pltpu.make_async_copy(pk_ref, k_own, load.at[0]),
+        pltpu.make_async_copy(pv_ref, v_own, load.at[1]),
         pltpu.make_async_copy(q_ref, qbuf.at[0], load.at[2]),
         pltpu.make_async_copy(ck_hbm, ck, load.at[3]),
         pltpu.make_async_copy(cv_hbm, cv, load.at[4]),
@@ -144,61 +136,44 @@
     for item in loads[3:]:
         item.start()
 
-    def put_keys(dst, at, rows):
-        size = rows.shape[0]
-        dst[at : at + size, 0:HD] = rows
-        dst[at : at + size, HD : 2 * HD] = rows
-
-    put_keys(k_own, 0, k_raw[...])
-    v_own[:, 0:HD] = v_raw[...]
-    v_own[:, HD : 2 * HD] = jnp.ones((prompt, HD), BF)
-    v_par[:, HD : 2 * HD] = jnp.ones((v_par.shape[0], HD), BF)
-
-    spans = [pl.ds(0, half), pl.ds(half, half)]
+    rows = tokens * HEADS_DEV
 
     def queries_of(i):
-        halves = []
-        for b in range(2):
-            heads = range(b * half_heads, (b + 1) * half_heads)
-            halves.append(split_query(jnp.concatenate([qbuf[i, :, h * HD : (h + 1) * HD] for h in heads], axis=0)))
-        return halves
+        return jnp.concatenate([qbuf[i, :, h * HD : (h + 1) * HD] for h in range(HEADS_DEV)], axis=0)
 
     def attend_own(i):
-        results = []
-        for queries in queries_of(i):
-            scores = dot_nt(queries, k_own[...])
-            top = jnp.max(scores, axis=1, keepdims=True)
-            results.append((top, dot_nn(jnp.exp2(scores - top).astype(BF), v_own[...])))
-        for at, (top, out) in zip(spans, results):
-            mx[i, at, :] = jnp.broadcast_to(top, (half, HD))
-            acc[i, at, :] = out[:, 0:HD]
-            sm[i, at, :] = out[:, HD : 2 * HD]
+        scores = dot_nt(queries_of(i), k_own[...])
+        top = jnp.max(scores, axis=1, keepdims=True)
+        weights = jnp.exp2((scores - top) * SCALE2)
+        total = jnp.sum(weights, axis=1, keepdims=True)
+        out = dot_nn(weights.astype(BF), v_own[...])
+        mx[i] = jnp.broadcast_to(top, (rows, HD))
+        sm[i] = jnp.broadcast_to(total, (rows, HD))
+        acc[i] = out
 
     def attend_partner(i):
         query_ctx = y_hi * ring + source_z(i)
         partner = (1 - y_hi) * ring + z
-        token = low_bits(lax.broadcasted_iota(jnp.int32, (half, 2 * tokens), 0), tokens)
-        key = lax.broadcasted_iota(jnp.int32, (half, 2 * tokens), 1)
+        token = low_bits(lax.broadcasted_iota(jnp.int32, (rows, 2 * tokens), 0), tokens)
+        key = lax.broadcasted_iota(jnp.int32, (rows, 2 * tokens), 1)
         key_pos = jnp.where(key < tokens, me * tokens + key, partner * tokens + key - tokens)
         visible = key_pos <= query_ctx * tokens + token
-        befores = [mx[i, at, 0:1] for at in spans]
-        results = []
-        for queries, before in zip(queries_of(i), befores):
-            scores = dot_nt(queries, k_par[...])
-            seen = jnp.where(visible, scores[:, prompt:], NEG)
-            top = jnp.maximum(
-                jnp.max(scores[:, 0:prompt], axis=1, keepdims=True), jnp.max(seen, axis=1, keepdims=True)
-            )
-            top = jnp.maximum(top, before)
-            weights = jnp.concatenate(
-                [jnp.exp2(scores[:, 0:prompt] - top).astype(BF), jnp.exp2(seen - top).astype(BF)], axis=1
-            )
-            results.append((top, dot_nn(weights, v_par[...])))
-        for at, before, (top, out) in zip(spans, befores, results):
-            keep = jnp.exp2(before - top)
-            mx[i, at, :] = jnp.broadcast_to(top, (half, HD))
-            acc[i, at, :] = acc[i, at, :] * keep + out[:, 0:HD]
-            sm[i, at, :] = sm[i, at, :] * keep + out[:, HD : 2 * HD]
+        before = mx[i, :, 0:1]
+        scores = dot_nt(queries_of(i), k_par[...])
+        seen = jnp.where(visible, scores[:, prompt:], NEG)
+        top = jnp.maximum(
+            jnp.max(scores[:, 0:prompt], axis=1, keepdims=True), jnp.max(seen, axis=1, keepdims=True)
+        )
+        top = jnp.maximum(top, before)
+        weights = jnp.concatenate(
+            [jnp.exp2((scores[:, 0:prompt] - top) * SCALE2), jnp.exp2((seen - top) * SCALE2)], axis=1
+        )
+        total = jnp.sum(weights, axis=1, keepdims=True)
+        out = dot_nn(weights.astype(BF), v_par[...])
+        keep = jnp.exp2((before - top) * SCALE2)
+        mx[i] = jnp.broadcast_to(top, (rows, HD))
+        sm[i] = sm[i] * keep + total
+        acc[i] = acc[i] * keep + out
 
     def own_step(n, carry):
         for c in range(2):
@@ -361,20 +336,14 @@
 
     span_relay().wait_recv()
     span = 2 * tokens
-    put_keys(k_par, prompt, jnp.concatenate([sk_ref[...], skv_par[0:tokens, :]], axis=0))
-    v_par[prompt : prompt + tokens, 0:HD] = sv_ref[...]
-    v_par[prompt + tokens : prompt + span, 0:HD] = skv_par[tokens:span, :]
+    k_par[prompt : prompt + tokens, :] = sk_ref[...]
+    k_par[prompt + tokens : prompt + span, :] = skv_par[0:tokens, :]
+    v_par[prompt : prompt + tokens, :] = sv_ref[...]
+    v_par[prompt + tokens : prompt + span, :] = skv_par[tokens:span, :]
     for j in range(parts):
         add_cores(1, j)
     for p in range(PIECES):
         piece_relay(p).wait_recv()
-        at = piece_rows(p)
-        if (p // 2) % 2 == 0:
-            put_keys(k_par, at, par[p])
-        else:
-            v_par[at : at + chunk, 0:HD] = par[p]
-
-    rows = 2 * half
 
     def out_copy(i):
         return remote(obuf.at[i], oin.at[i], o_send.at[i], o_recv.at[i], back(i))
@@ -390,8 +359,8 @@
             in_m[at : at + 8, :] = jnp.broadcast_to(stats[:, a : a + 1], (8, HD))
             in_l[at : at + 8, :] = jnp.broadcast_to(stats[:, a + 8 : a + 9], (8, HD))
         top = jnp.maximum(mx[i], in_m[...])
-        keep = jnp.exp2(mx[i] - top)
-        add = jnp.exp2(in_m[...] - top)
+        keep = jnp.exp2((mx[i] - top) * SCALE2)
+        add = jnp.exp2((in_m[...] - top) * SCALE2)
         acc[i] = acc[i] * keep + oin[box, 0:rows, :].astype(F32) * add
         sm[i] = sm[i] * keep + in_l[...] * add
         mx[i] = top
@@ -512,13 +481,10 @@
             pltpu.VMEM((span, HD), BF),
             pltpu.VMEM((ring, 2, span, HD), BF),
             pltpu.VMEM((PIECES, prompt // 4, HD), BF),
-            pltpu.VMEM((PIECES, prompt // 4, HD), BF),
             pltpu.VMEM((prompt, HD), BF),
             pltpu.VMEM((prompt, HD), BF),
-            pltpu.VMEM((prompt, 2 * HD), BF),
-            pltpu.VMEM((prompt, 2 * HD), BF),
-            pltpu.VMEM((total, 2 * HD), BF),
-            pltpu.VMEM((total, 2 * HD), BF),
+            pltpu.VMEM((total, HD), BF),
+            pltpu.VMEM((total, HD), BF),
             pltpu.VMEM((ring, rows, HD), F32),
             pltpu.VMEM((ring, rows, HD), F32),
             pltpu.VMEM((ring, rows, HD), F32),

time: 74.3 us -> 80.8 us (1.087)
  Pallas kernels: 73.5 us -> 80 us
    pallas_call x1, Pallas kernels: 72 us -> 78.4 us  [on_device(): pl.pallas_call(lambda *refs: kernel(ring, tp_count, *refs), out_shape=jax...]
where the time goes in v6:
time: 80.8 us; the launch traced here: 80.6 us
  Pallas kernels  80 us (99%)
    pallas_call x1, Pallas kernels, on_device(): pl.pallas_call(lambda *refs: kernel(ring, tp_count, *refs), out_shape=jax...  78.4 us

profile of v6, /device:TPU:1, one launch (start us, length us, event | category | flops | bytes accessed | tf_op | source)
XLA Modules:
  0.0 80.6 jit_solution(16120331343979663819)
XLA Ops:
  0.6 78.4 %serve.1.sums_ref = bf16[16,4096]{1,0:T(8,128)(2,1)} custom-call(bf16[64,1024]{1,0:T(8,128)(2,1)} %bitcast.16, bf16[64,128]{1,0:T(8,128)(2,1)} %bitcast.18, bf16[64,128]{1,0:T(8,128)(2,1)} %bitcast.19, bf16[2048,128]{1,0:T(8,128)(2,1)} %bitcast.14, bf16[2048,128]{1,0:T(8,128)(2,1)} %bitcast.15, s32[2,64]{1,0:T(2,128)} %refs_5_.1, s32[2,64]{1,0:T(2,128)} %refs_6_.1, ...), custom_call_target="tpu_custom_call" | custom-call | tf_op jit(solution)/shard_map/serve/pallas_call | solution.py:473
  79.1 1.6 %separate.1 = (bf16[8,4096]{1,0:T(8,128)(2,1)}, bf16[2,4,4096]{2,1,0:T(4,128)(2,1)}) custom-call(bf16[16,4096]{1,0:T(8,128)(2,1)} %serve.1.sums_ref), custom_call_target="tpu_custom_call" | custom-call | tf_op jit(solution)/shard_map/separate/pallas_call | solution.py:543

commit v7 on v5

--- a/solution.py
+++ b/solution.py
@@ -12,6 +12,8 @@
 SLOTS = 8
 HEADS_DEV = 8
 PIECES = 8
+TILE = 256
+ROWS = 64
 NEG = -1e30
 SCALE2 = HD**-0.5 * math.log2(math.e)
 MESH = pl.DeviceIdType.MESH
@@ -46,7 +48,7 @@
     ring, tp_count,
     q_ref, sk_ref, sv_ref, pk_ref, pv_ref, owner_ref, slot_ref, dq_ref, dk_ref, dv_ref, ck_hbm, cv_hbm, len_ref, w_hbm,
     out_ref,
-    qbuf, skv, skv_par, gath, rel, par, k_raw, v_raw, k_own, v_own, k_par, v_par,
+    qbuf, skv, skv_par, gath, rel, par, k_raw, v_raw, k_own, v_own, k_par, v_par, raised, shares,
     acc, mx, sm, in_m, in_l, obuf, oin,
     w, ck, cv, att, part, sib, pairs, got,
     q_send, q_recv, s_send, s_recv, sp_send, sp_recv, g_send, g_recv, r_send, r_recv, f_send, f_recv,
@@ -146,10 +148,12 @@
 
     def put_keys(dst, at, rows):
         size = rows.shape[0]
-        dst[at : at + size, 0:HD] = rows
-        dst[at : at + size, HD : 2 * HD] = rows
-
-    put_keys(k_own, 0, k_raw[...])
+        turned = rows.T
+        dst[0:HD, at : at + size] = turned
+        dst[HD : 2 * HD, at : at + size] = turned
+
+    for c in range(4):
+        put_keys(k_own, c * chunk, k_raw[c * chunk : (c + 1) * chunk])
     v_own[:, 0:HD] = v_raw[...]
     v_own[:, HD : 2 * HD] = jnp.ones((prompt, HD), BF)
     v_par[:, HD : 2 * HD] = jnp.ones((v_par.shape[0], HD), BF)
@@ -163,42 +167,68 @@
             halves.append(split_query(jnp.concatenate([qbuf[i, :, h * HD : (h + 1) * HD] for h in heads], axis=0)))
         return halves
 
-    def attend_own(i):
-        results = []
-        for queries in queries_of(i):
-            scores = dot_nt(queries, k_own[...])
-            top = jnp.max(scores, axis=1, keepdims=True)
-            results.append((top, dot_nn(jnp.exp2(scores - top).astype(BF), v_own[...])))
-        for at, (top, out) in zip(spans, results):
-            mx[i, at, :] = jnp.broadcast_to(top, (half, HD))
-            acc[i, at, :] = out[:, 0:HD]
-            sm[i, at, :] = out[:, HD : 2 * HD]
-
-    def attend_partner(i):
-        query_ctx = y_hi * ring + source_z(i)
-        partner = (1 - y_hi) * ring + z
-        token = low_bits(lax.broadcasted_iota(jnp.int32, (half, 2 * tokens), 0), tokens)
-        key = lax.broadcasted_iota(jnp.int32, (half, 2 * tokens), 1)
-        key_pos = jnp.where(key < tokens, me * tokens + key, partner * tokens + key - tokens)
-        visible = key_pos <= query_ctx * tokens + token
-        befores = [mx[i, at, 0:1] for at in spans]
-        results = []
-        for queries, before in zip(queries_of(i), befores):
-            scores = dot_nt(queries, k_par[...])
-            seen = jnp.where(visible, scores[:, prompt:], NEG)
-            top = jnp.maximum(
-                jnp.max(scores[:, 0:prompt], axis=1, keepdims=True), jnp.max(seen, axis=1, keepdims=True)
-            )
-            top = jnp.maximum(top, before)
-            weights = jnp.concatenate(
-                [jnp.exp2(scores[:, 0:prompt] - top).astype(BF), jnp.exp2(seen - top).astype(BF)], axis=1
-            )
-            results.append((top, dot_nn(weights, v_par[...])))
-        for at, before, (top, out) in zip(spans, befores, results):
-            keep = jnp.exp2(before - top)
-            mx[i, at, :] = jnp.broadcast_to(top, (half, HD))
-            acc[i, at, :] = acc[i, at, :] * keep + out[:, 0:HD]
-            sm[i, at, :] = sm[i, at, :] * keep + out[:, HD : 2 * HD]
+    def attend(i, keys, values, span):
+        total = keys.shape[1]
+        tiles = [(a, min(TILE, total - a)) for a in range(0, total, TILE)]
+        queries = queries_of(i)
+        befores = [mx[i, at, 0:1] for at in spans] if span else None
+        top = [None, None]
+        out = [None, None]
+
+        def score(b, a, size):
+            s = dot_nn(queries[b], keys[:, a : a + size])
+            if span and a == prompt:
+                query_ctx = y_hi * ring + source_z(i)
+                partner = (1 - y_hi) * ring + z
+                token = low_bits(lax.broadcasted_iota(jnp.int32, (half, 2 * tokens), 0), tokens)
+                key = lax.broadcasted_iota(jnp.int32, (half, 2 * tokens), 1)
+                key_pos = jnp.where(key < tokens, me * tokens + key, partner * tokens + key - tokens)
+                s = jnp.where(key_pos <= query_ctx * tokens + token, s, NEG)
+            raised[b, :, a : a + size] = s
+            for c in range(0, size, HD):
+                piece = s[:, c : c + HD]
+                top[b] = piece if top[b] is None else jnp.maximum(top[b], piece)
+
+        def settle(b):
+            top[b] = jnp.max(top[b], axis=1, keepdims=True)
+            if span:
+                top[b] = jnp.maximum(top[b], befores[b])
+
+        def weigh(b, a, size):
+            for r in range(0, half, ROWS):
+                less = raised[b, r : r + ROWS, a : a + size] - top[b][r : r + ROWS]
+                shares[b, r : r + ROWS, a : a + size] = jnp.exp2(less).astype(BF)
+
+        def blend(b, a, end):
+            piece = dot_nn(shares[b, :, a:end], values[a:end, :])
+            out[b] = piece if out[b] is None else out[b] + piece
+
+        middle = len(tiles) // 2
+        cut = tiles[middle][0]
+        for tile in tiles:
+            score(0, *tile)
+        settle(0)
+        for tile in tiles:
+            score(1, *tile)
+            weigh(0, *tile)
+        settle(1)
+        blend(0, 0, cut)
+        for tile in tiles[:middle]:
+            weigh(1, *tile)
+        blend(0, cut, total)
+        blend(1, 0, cut)
+        for tile in tiles[middle:]:
+            weigh(1, *tile)
+        blend(1, cut, total)
+        for b, at in enumerate(spans):
+            if span:
+                keep = jnp.exp2(befores[b] - top[b])
+                acc[i, at, :] = acc[i, at, :] * keep + out[b][:, 0:HD]
+                sm[i, at, :] = sm[i, at, :] * keep + out[b][:, HD : 2 * HD]
+            else:
+                acc[i, at, :] = out[b][:, 0:HD]
+                sm[i, at, :] = out[b][:, HD : 2 * HD]
+            mx[i, at, :] = jnp.broadcast_to(top[b], (half, HD))
 
     def own_step(n, carry):
         for c in range(2):
@@ -210,7 +240,7 @@
             def _():
                 query_copy(n + c + 2, qbuf.at[n + c]).start()
 
-        attend_own(n)
+        attend(n, k_own, v_own, False)
 
         @pl.when(n == 0)
         def _():
@@ -411,7 +441,7 @@
 
     def partner_step(m, carry):
         i = ring - 1 - m
-        attend_partner(i)
+        attend(i, k_par, v_par, True)
 
         @pl.when(i + 2 < ring)
         def _():
@@ -422,7 +452,7 @@
         return carry
 
     lax.fori_loop(0, ring - 1, partner_step, 0)
-    attend_partner(0)
+    attend(0, k_par, v_par, True)
     merge(0, 2)
     merge(0, 1)
     done = (acc[0] / sm[0]).astype(BF)
@@ -515,10 +545,12 @@
             pltpu.VMEM((PIECES, prompt // 4, HD), BF),
             pltpu.VMEM((prompt, HD), BF),
             pltpu.VMEM((prompt, HD), BF),
+            pltpu.VMEM((2 * HD, prompt), BF),
             pltpu.VMEM((prompt, 2 * HD), BF),
-            pltpu.VMEM((prompt, 2 * HD), BF),
+            pltpu.VMEM((2 * HD, total), BF),
             pltpu.VMEM((total, 2 * HD), BF),
-            pltpu.VMEM((total, 2 * HD), BF),
+            pltpu.VMEM((2, rows // 2, total), F32),
+            pltpu.VMEM((2, rows // 2, total), BF),
             pltpu.VMEM((ring, rows, HD), F32),
             pltpu.VMEM((ring, rows, HD), F32),
             pltpu.VMEM((ring, rows, HD), F32),

time: 74.3 us -> 71.7 us (0.965)
  Pallas kernels: 73.5 us -> 71 us
    pallas_call x1, Pallas kernels: 72 us -> 69.4 us  [on_device(): pl.pallas_call(lambda *refs: kernel(ring, tp_count, *refs), out_shape=jax...]
where the time goes in v7:
time: 71.7 us; the launch traced here: 71.6 us
  Pallas kernels  71 us (99%)
    pallas_call x1, Pallas kernels, on_device(): pl.pallas_call(lambda *refs: kernel(ring, tp_count, *refs), out_shape=jax...  69.4 us
    pallas_call x1, Pallas kernels, on_device(): pl.pallas_call(separate, out_shape=(jax.ShapeDtypeStruct((each, columns),...  1.57 us

profile of v7, /device:TPU:1, one launch (start us, length us, event | category | flops | bytes accessed | tf_op | source)
XLA Modules:
  0.0 71.6 jit_solution(16708436721264132561)
XLA Ops:
  0.6 69.4 %serve.1.sums_ref = bf16[16,4096]{1,0:T(8,128)(2,1)} custom-call(bf16[64,1024]{1,0:T(8,128)(2,1)} %bitcast.16, bf16[64,128]{1,0:T(8,128)(2,1)} %bitcast.18, bf16[64,128]{1,0:T(8,128)(2,1)} %bitcast.19, bf16[2048,128]{1,0:T(8,128)(2,1)} %bitcast.14, bf16[2048,128]{1,0:T(8,128)(2,1)} %bitcast.15, s32[2,64]{1,0:T(2,128)} %refs_5_.1, s32[2,64]{1,0:T(2,128)} %refs_6_.1, ...), custom_call_target="tpu_custom_call" | custom-call | tf_op jit(solution)/shard_map/serve/pallas_call | solution.py:534
  70.0 1.6 %separate.1 = (bf16[8,4096]{1,0:T(8,128)(2,1)}, bf16[2,4,4096]{2,1,0:T(4,128)(2,1)}) custom-call(bf16[16,4096]{1,0:T(8,128)(2,1)} %serve.1.sums_ref), custom_call_target="tpu_custom_call" | custom-call | tf_op jit(solution)/shard_map/separate/pallas_call | solution.py:609

commit v8 on v7

--- a/solution.py
+++ b/solution.py
@@ -160,25 +160,24 @@
 
     spans = [pl.ds(0, half), pl.ds(half, half)]
 
-    def queries_of(i):
-        halves = []
-        for b in range(2):
-            heads = range(b * half_heads, (b + 1) * half_heads)
-            halves.append(split_query(jnp.concatenate([qbuf[i, :, h * HD : (h + 1) * HD] for h in heads], axis=0)))
-        return halves
-
-    def attend(i, keys, values, span):
+    def queries_of(i, b):
+        heads = range(b * half_heads, (b + 1) * half_heads)
+        return split_query(jnp.concatenate([qbuf[i, :, h * HD : (h + 1) * HD] for h in heads], axis=0))
+
+    def attend(shards, keys, values, span):
         total = keys.shape[1]
         tiles = [(a, min(TILE, total - a)) for a in range(0, total, TILE)]
-        queries = queries_of(i)
-        befores = [mx[i, at, 0:1] for at in spans] if span else None
-        top = [None, None]
-        out = [None, None]
+        halves = [(i, b) for i in shards for b in range(2)]
+        count = len(halves)
+        queries = [queries_of(i, b) for i, b in halves]
+        befores = [mx[i, spans[b], 0:1] for i, b in halves] if span else None
+        top = [None] * count
+        out = [None] * count
 
         def score(b, a, size):
             s = dot_nn(queries[b], keys[:, a : a + size])
             if span and a == prompt:
-                query_ctx = y_hi * ring + source_z(i)
+                query_ctx = y_hi * ring + source_z(halves[b][0])
                 partner = (1 - y_hi) * ring + z
                 token = low_bits(lax.broadcasted_iota(jnp.int32, (half, 2 * tokens), 0), tokens)
                 key = lax.broadcasted_iota(jnp.int32, (half, 2 * tokens), 1)
@@ -205,69 +204,77 @@
 
         middle = len(tiles) // 2
         cut = tiles[middle][0]
-        for tile in tiles:
-            score(0, *tile)
-        settle(0)
-        for tile in tiles:
-            score(1, *tile)
-            weigh(0, *tile)
-        settle(1)
-        blend(0, 0, cut)
+        for p in range(count):
+            for c, tile in enumerate(tiles):
+                score(p, *tile)
+                if p >= 1:
+                    weigh(p - 1, *tile)
+                if p >= 2 and c == 0:
+                    blend(p - 2, 0, cut)
+                if p >= 2 and c == middle:
+                    blend(p - 2, cut, total)
+            settle(p)
+        blend(count - 2, 0, cut)
         for tile in tiles[:middle]:
-            weigh(1, *tile)
-        blend(0, cut, total)
-        blend(1, 0, cut)
+            weigh(count - 1, *tile)
+        blend(count - 2, cut, total)
+        blend(count - 1, 0, cut)
         for tile in tiles[middle:]:
-            weigh(1, *tile)
-        blend(1, cut, total)
-        for b, at in enumerate(spans):
+            weigh(count - 1, *tile)
+        blend(count - 1, cut, total)
+        for h, (i, b) in enumerate(halves):
+            at = spans[b]
             if span:
-                keep = jnp.exp2(befores[b] - top[b])
-                acc[i, at, :] = acc[i, at, :] * keep + out[b][:, 0:HD]
-                sm[i, at, :] = sm[i, at, :] * keep + out[b][:, HD : 2 * HD]
+                keep = jnp.exp2(befores[h] - top[h])
+                acc[i, at, :] = acc[i, at, :] * keep + out[h][:, 0:HD]
+                sm[i, at, :] = sm[i, at, :] * keep + out[h][:, HD : 2 * HD]
             else:
-                acc[i, at, :] = out[b][:, 0:HD]
-                sm[i, at, :] = out[b][:, HD : 2 * HD]
-            mx[i, at, :] = jnp.broadcast_to(top[b], (half, HD))
-
-    def own_step(n, carry):
-        for c in range(2):
-            @pl.when(jnp.logical_and(n % 2 == 1, n + c < ring))
+                acc[i, at, :] = out[h][:, 0:HD]
+                sm[i, at, :] = out[h][:, HD : 2 * HD]
+            mx[i, at, :] = jnp.broadcast_to(top[h], (half, HD))
+
+    def own_step(k, carry):
+        for c in range(1, 3):
+            m = 2 * k + c
+
+            @pl.when(m < ring)
             def _():
-                query_copy(n + c, qbuf.at[0]).wait_recv()
-
-            @pl.when(jnp.logical_and(n % 2 == 1, n + c + 2 < ring))
+                query_copy(m, qbuf.at[0]).wait_recv()
+
+            @pl.when(m + 2 < ring)
             def _():
-                query_copy(n + c + 2, qbuf.at[n + c]).start()
-
-        attend(n, k_own, v_own, False)
-
-        @pl.when(n == 0)
+                query_copy(m + 2, qbuf.at[m]).start()
+
+        @pl.when(k == 0)
         def _():
-            for k in range(2):
-                span_copy(k).wait_recv()
+            for c in range(2):
+                span_copy(c).wait_recv()
             span_relay().start()
             gather_copy(1, z).start()
             gather_copy(2, z).start()
 
+        attend((2 * k, 2 * k + 1), k_own, v_own, False)
+
         for c in range(PIECES // 2):
-            @pl.when(n == min(c + 2, ring - 1))
+            @pl.when(k == min(c, ring // 2 - 1, 2))
             def _():
                 forward_piece(2 * c)
                 forward_piece(2 * c + 1)
 
-        @pl.when(n > 0)
-        def _():
-            at = source_z(n)
-            gather_copy(n, at).wait_recv()
-
-            @pl.when(n + 2 < ring)
+        for c in range(1, 3):
+            m = 2 * k + c
+
+            @pl.when(m < ring)
             def _():
-                gather_copy(n + 2, at).start()
+                gather_copy(m, source_z(m)).wait_recv()
+
+            @pl.when(m + 2 < ring)
+            def _():
+                gather_copy(m + 2, source_z(m)).start()
 
         return carry
 
-    lax.fori_loop(0, ring, own_step, 0)
+    lax.fori_loop(0, ring // 2, own_step, 0)
 
     each = tokens // tp_count
     parts = part.shape[1]
@@ -440,19 +447,23 @@
         ).astype(BF)
 
     def partner_step(m, carry):
-        i = ring - 1 - m
-        attend(i, k_par, v_par, True)
-
-        @pl.when(i + 2 < ring)
-        def _():
-            merge(i, i + 2)
-
-        pack(i)
-        out_copy(i).start()
+        k = ring // 2 - 1 - m
+        attend((2 * k + 1, 2 * k), k_par, v_par, True)
+        for i in (2 * k + 1, 2 * k):
+            @pl.when(i + 2 < ring)
+            def _():
+                merge(i, i + 2)
+
+            pack(i)
+            out_copy(i).start()
         return carry
 
-    lax.fori_loop(0, ring - 1, partner_step, 0)
-    attend(0, k_par, v_par, True)
+    lax.fori_loop(0, ring // 2 - 1, partner_step, 0)
+    attend((1,), k_par, v_par, True)
+    merge(1, 3)
+    pack(1)
+    out_copy(1).start()
+    attend((0,), k_par, v_par, True)
     merge(0, 2)
     merge(0, 1)
     done = (acc[0] / sm[0]).astype(BF)
@@ -549,8 +560,8 @@
             pltpu.VMEM((prompt, 2 * HD), BF),
             pltpu.VMEM((2 * HD, total), BF),
             pltpu.VMEM((total, 2 * HD), BF),
-            pltpu.VMEM((2, rows // 2, total), F32),
-            pltpu.VMEM((2, rows // 2, total), BF),
+            pltpu.VMEM((4, rows // 2, total), F32),
+            pltpu.VMEM((4, rows // 2, total), BF),
             pltpu.VMEM((ring, rows, HD), F32),
             pltpu.VMEM((ring, rows, HD), F32),
             pltpu.VMEM((ring, rows, HD), F32),

time: 71.7 us -> 74.6 us (1.040)
  Pallas kernels: 71 us -> 73.9 us
    pallas_call x1, Pallas kernels: 69.4 us -> 72.3 us  [on_device(): pl.pallas_call(lambda *refs: kernel(ring, tp_count, *refs), out_shape=jax...]
where the time goes in v8:
time: 74.6 us; the launch traced here: 74.5 us
  Pallas kernels  73.9 us (99%)
    pallas_call x1, Pallas kernels, on_device(): pl.pallas_call(lambda *refs: kernel(ring, tp_count, *refs), out_shape=jax...  72.3 us
    pallas_call x1, Pallas kernels, on_device(): pl.pallas_call(separate, out_shape=(jax.ShapeDtypeStruct((each, columns),...  1.57 us

profile of v8, /device:TPU:1, one launch (start us, length us, event | category | flops | bytes accessed | tf_op | source)
XLA Modules:
  0.0 74.5 jit_solution(11078748166046376857)
XLA Ops:
  0.6 72.3 %serve.1.sums_ref = bf16[16,4096]{1,0:T(8,128)(2,1)} custom-call(bf16[64,1024]{1,0:T(8,128)(2,1)} %bitcast.16, bf16[64,128]{1,0:T(8,128)(2,1)} %bitcast.18, bf16[64,128]{1,0:T(8,128)(2,1)} %bitcast.19, bf16[2048,128]{1,0:T(8,128)(2,1)} %bitcast.14, bf16[2048,128]{1,0:T(8,128)(2,1)} %bitcast.15, s32[2,64]{1,0:T(2,128)} %refs_5_.1, s32[2,64]{1,0:T(2,128)} %refs_6_.1, ...), custom_call_target="tpu_custom_call" | custom-call | tf_op jit(solution)/shard_map/serve/pallas_call | solution.py:545
  72.9 1.6 %separate.1 = (bf16[8,4096]{1,0:T(8,128)(2,1)}, bf16[2,4,4096]{2,1,0:T(4,128)(2,1)}) custom-call(bf16[16,4096]{1,0:T(8,128)(2,1)} %serve.1.sums_ref), custom_call_target="tpu_custom_call" | custom-call | tf_op jit(solution)/shard_map/separate/pallas_call | solution.py:620
